TPU v7x, 32 devices: a whole 2x2x4 slice. The times are simulated.
32 devices in a mesh: dp: 16 (over z, x, core), tensor: 2 (over y).
Axes of the slice: x: 2, y: 2, z: 4, core: 2. Of those that a mesh axis runs over, the one named last changes fastest.
Arguments:
- tokens: bfloat16 [512, 32, 1536], P('tensor', 'dp'), may hold values from -6 to 6
- cached_len: int32 [32], P('dp'), may hold values from 0 to 32768, as said below
- prompt_group: int32 [32], P('dp'), may hold values from 0 to 7, as said below
- attn_gain: float32 [1536], replicated, may hold values from 0.1 to 1.9
- w_query: bfloat16 [1536, 1536], P(None, 'tensor'), may hold values from -0.15625 to 0.15625
- key_matrix: bfloat16 [1536, 768], P(None, 'tensor'), may hold values from -0.15625 to 0.15625
- value_matrix: bfloat16 [1536, 768], P(None, 'tensor'), may hold values from -0.15625 to 0.15625
- w_out: bfloat16 [1536, 1536], P('tensor'), may hold values from -1.25 to 1.25
- window_cache_keys: bfloat16 [32, 4096, 768], P('dp', None, 'tensor'), may hold values from -400 to 400
- window_cache_values: bfloat16 [32, 4096, 768], P('dp', None, 'tensor'), may hold values from -6 to 6
- prompt_keys: bfloat16 [8, 4096, 768], P(None, 'dp', 'tensor'), may hold values from -6 to 6
- prompt_values: bfloat16 [8, 4096, 768], P(None, 'dp', 'tensor'), may hold values from -6 to 6
- mlp_gain: float32 [1536], replicated, may hold values from 0.1 to 1.9
- w_gate: bfloat16 [1536, 4096], P(None, 'tensor'), may hold values from -0.15625 to 0.15625
- w_up: bfloat16 [1536, 4096], P(None, 'tensor'), may hold values from -0.15625 to 0.15625
- w_down: bfloat16 [4096, 1536], P('tensor'), may hold values from -0.09375 to 0.09375
Outputs:
- output: bfloat16 [512, 32, 1536], P('tensor', 'dp')
Inputs may be any that keep to these rules, and one draw needn't show every extreme that they name: `cached_len`: in each prompt group some request has no cached tokens, and exactly one request in all has 32768. `prompt_group`: every group holds 4 requests.
All inputs are finite; a program needn't handle non-finite values.
Results may differ from a plain program's by a relative error of at most 0.024.
Values may be sent and summed in bfloat16 or wider, within the bound.
No kernel may reach another device: no remote copies, remote signals or barrier semaphores. Data moves between devices by JAX's collectives and lax.ppermute only.
A program may use at most 192 MiB of HBM per device.

v0:
```python
import math

import jax
import jax.numpy as jnp
from jax import lax
from jax.sharding import PartitionSpec as P

MODEL_WIDTH = 1536
HEAD_SIZE = 96
FRESH_TOKENS = 512
WINDOW_SPAN = 4096
SINKS = 4
PROMPT_TOKENS = 4096


rope_base = 10000.0
epsilon = 1e-05
far_below = -1e30


def norm_rows(values, gain_vec):
    widened = values.astype(jnp.float32)
    factor = lax.rsqrt(jnp.mean(widened * widened, axis=-1, keepdims=True) + epsilon)
    return (widened * factor * gain_vec).astype(jnp.bfloat16)


def rotate(values, positions):
    half_dim = values.shape[-1] // 2
    frequency = rope_base ** (-2.0 * jnp.arange(half_dim, dtype=jnp.float32) / values.shape[-1])
    angles = positions.astype(jnp.float32)[..., None, None] * frequency
    cosine = jnp.cos(angles)
    sine_part = jnp.sin(angles)
    first_half = values[..., :half_dim]
    second_half = values[..., half_dim:]
    return jnp.concatenate(
        [
            first_half * cosine - second_half * sine_part,
            second_half * cosine + first_half * sine_part,
        ],
        axis=-1,
    )


def absorb(soft_state, queries, key_block, value_block, visible, score_scale):
    row_peak, row_sum, accumulated = soft_state
    scores = (
        jnp.einsum("irhgd,rkhd->rhgik", queries, key_block, preferred_element_type=jnp.float32)
        * score_scale
    )
    scores = jnp.where(visible[:, None, None], scores, -jnp.inf)
    new_peak = jnp.maximum(row_peak, jnp.max(scores, axis=-1))
    factor = jnp.exp(row_peak - new_peak)
    weights = jnp.exp(scores - new_peak[..., None])
    blended = jnp.einsum(
        "rhgik,rkhd->rhgid",
        weights.astype(jnp.bfloat16),
        value_block,
        preferred_element_type=jnp.float32,
    )
    return (
        new_peak,
        row_sum * factor + jnp.sum(weights, axis=-1),
        accumulated * factor[..., None] + blended,
    )


def shared_block(soft_state, pieces, queries, selector, horizon, score_scale):
    key_piece, value_piece = pieces
    row_count = key_piece.shape[1]
    key_heads = key_piece.shape[2] // HEAD_SIZE
    local_reqs = queries.shape[1]
    picked_keys = jnp.take(key_piece, selector, axis=0).reshape(
        local_reqs, row_count, key_heads, HEAD_SIZE
    )
    picked_values = jnp.take(value_piece, selector, axis=0).reshape(
        local_reqs, row_count, key_heads, HEAD_SIZE
    )
    block_len = math.gcd(row_count, FRESH_TOKENS)

    def block_step(running, block_index):
        block_start = block_index * block_len
        key_block = lax.dynamic_slice_in_dim(picked_keys, block_start, block_len, 1)
        value_block = lax.dynamic_slice_in_dim(picked_values, block_start, block_len, 1)
        prompt_pos = block_start + jnp.arange(block_len, dtype=jnp.int32)
        visible = (prompt_pos[None, None, :] < SINKS) | (
            prompt_pos[None, None, :] > horizon[:, :, None]
        )
        return (absorb(running, queries, key_block, value_block, visible, score_scale), None)

    return lax.scan(block_step, soft_state, jnp.arange(row_count // block_len, dtype=jnp.int32))[0]


def body(
    tokens,
    cached_len,
    prompt_group,
    attn_gain,
    w_query,
    key_matrix,
    value_matrix,
    w_out,
    window_cache_keys,
    window_cache_values,
    prompt_keys,
    prompt_values,
    mlp_gain,
    w_gate,
    w_up,
    w_down,
):
    local_rows = tokens.shape[0]
    local_reqs = tokens.shape[1]
    query_cols = w_query.shape[1]
    key_cols = key_matrix.shape[1]
    hidden_cols = w_gate.shape[1]
    key_heads = key_cols // HEAD_SIZE
    query_group_width = query_cols // key_cols
    score_scale = 1.0 / math.sqrt(HEAD_SIZE)
    source = norm_rows(tokens, attn_gain)
    offset = 0
    row_piece = lax.all_gather(source, "tensor", axis=0, tiled=True)
    row_count = row_piece.shape[0]
    normed = row_piece
    flattened_rows = normed.reshape(row_count * local_reqs, MODEL_WIDTH)
    positions = (
        PROMPT_TOKENS + cached_len[None, :] + jnp.arange(row_count, dtype=jnp.int32)[:, None]
    )
    project_queries = jnp.dot(flattened_rows, w_query, preferred_element_type=jnp.float32).reshape(
        row_count, local_reqs, query_cols // HEAD_SIZE, HEAD_SIZE
    )
    fresh_keys = jnp.dot(flattened_rows, key_matrix, preferred_element_type=jnp.float32).reshape(
        row_count, local_reqs, key_heads, HEAD_SIZE
    )
    fresh_values = (
        jnp.dot(flattened_rows, value_matrix, preferred_element_type=jnp.float32)
        .astype(jnp.bfloat16)
        .reshape(row_count, local_reqs, key_cols)
    )
    project_queries = (
        rotate(project_queries, positions)
        .astype(jnp.bfloat16)
        .reshape(row_count, local_reqs, query_cols)
    )
    fresh_keys = (
        rotate(fresh_keys, positions).astype(jnp.bfloat16).reshape(row_count, local_reqs, key_cols)
    )
    gathered = jnp.concatenate([project_queries, fresh_keys, fresh_values], axis=2)
    queries = gathered[:, :, offset : offset + query_cols].reshape(
        FRESH_TOKENS, local_reqs, key_heads, query_group_width, HEAD_SIZE
    )
    own_keys = jnp.swapaxes(
        gathered[:, :, offset + query_cols : offset + query_cols + key_cols], 0, 1
    ).reshape(local_reqs, FRESH_TOKENS, key_heads, HEAD_SIZE)
    own_values = jnp.swapaxes(
        gathered[:, :, offset + query_cols + key_cols : offset + query_cols + 2 * key_cols], 0, 1
    ).reshape(local_reqs, FRESH_TOKENS, key_heads, HEAD_SIZE)
    state_shape = (local_reqs, key_heads, query_group_width, FRESH_TOKENS)
    soft_state = (
        jnp.full(state_shape, far_below, jnp.float32),
        jnp.zeros(state_shape, jnp.float32),
        jnp.zeros(state_shape + (HEAD_SIZE,), jnp.float32),
    )
    row_ids = jnp.arange(FRESH_TOKENS, dtype=jnp.int32)
    causal = jnp.broadcast_to(
        row_ids[None, None, :] <= row_ids[None, :, None], (local_reqs, FRESH_TOKENS, FRESH_TOKENS)
    )
    soft_state = absorb(soft_state, queries, own_keys, own_values, causal, score_scale)
    past_keys = window_cache_keys.reshape(local_reqs, WINDOW_SPAN, key_heads, HEAD_SIZE)
    past_values = window_cache_values.reshape(local_reqs, WINDOW_SPAN, key_heads, HEAD_SIZE)

    def window_step(running, block_index):
        block_start = block_index * FRESH_TOKENS
        key_block = lax.dynamic_slice_in_dim(past_keys, block_start, FRESH_TOKENS, 1)
        value_block = lax.dynamic_slice_in_dim(past_values, block_start, FRESH_TOKENS, 1)
        slot_ids = block_start + row_ids
        visible = (slot_ids[None, None, :] >= WINDOW_SPAN - cached_len[:, None, None]) & (
            slot_ids[None, None, :] > row_ids[None, :, None]
        )
        return (absorb(running, queries, key_block, value_block, visible, score_scale), None)

    soft_state = lax.scan(
        window_step, soft_state, jnp.arange(WINDOW_SPAN // FRESH_TOKENS, dtype=jnp.int32)
    )[0]
    horizon = PROMPT_TOKENS + cached_len[:, None] + row_ids[None, :] - WINDOW_SPAN
    soft_state = shared_block(
        soft_state,
        (
            lax.all_gather(prompt_keys, "dp", axis=1, tiled=True),
            lax.all_gather(prompt_values, "dp", axis=1, tiled=True),
        ),
        queries,
        prompt_group,
        horizon,
        score_scale,
    )
    row_peak, row_sum, accumulated = soft_state
    attended = (accumulated / row_sum[..., None]).astype(jnp.bfloat16)
    attended = attended.transpose(3, 0, 1, 2, 4).reshape(FRESH_TOKENS, local_reqs, query_cols)
    picked = attended
    attn_part = lax.psum_scatter(
        jnp.dot(
            picked.reshape(lax.axis_size("tensor") * local_rows * local_reqs, query_cols),
            w_out,
            preferred_element_type=jnp.float32,
        )
        .reshape(lax.axis_size("tensor") * local_rows, local_reqs, MODEL_WIDTH)
        .astype(jnp.bfloat16),
        "tensor",
        scatter_dimension=0,
        tiled=True,
    ).astype(jnp.float32)
    residual = (tokens.astype(jnp.float32) + attn_part).astype(jnp.bfloat16)
    row_piece = lax.all_gather(norm_rows(residual, mlp_gain), "tensor", axis=0, tiled=True)
    row_count = row_piece.shape[0]
    flattened_rows = row_piece.reshape(row_count * local_reqs, MODEL_WIDTH)
    gate_part = jnp.dot(flattened_rows, w_gate, preferred_element_type=jnp.float32)
    up_part = jnp.dot(flattened_rows, w_up, preferred_element_type=jnp.float32)
    hidden = (
        (jax.nn.silu(gate_part) * up_part)
        .astype(jnp.bfloat16)
        .reshape(row_count, local_reqs, hidden_cols)
    )
    picked = hidden
    mlp_part = lax.psum_scatter(
        jnp.dot(
            picked.reshape(lax.axis_size("tensor") * local_rows * local_reqs, hidden_cols),
            w_down,
            preferred_element_type=jnp.float32,
        )
        .reshape(lax.axis_size("tensor") * local_rows, local_reqs, MODEL_WIDTH)
        .astype(jnp.bfloat16),
        "tensor",
        scatter_dimension=0,
        tiled=True,
    ).astype(jnp.float32)
    return (residual.astype(jnp.float32) + mlp_part).astype(jnp.bfloat16)


def solution(mesh):
    in_specs = (
        P("tensor", "dp", None),
        P("dp"),
        P("dp"),
        P(),
        P(None, "tensor"),
        P(None, "tensor"),
        P(None, "tensor"),
        P("tensor", None),
        P("dp", None, "tensor"),
        P("dp", None, "tensor"),
        P(None, "dp", "tensor"),
        P(None, "dp", "tensor"),
        P(),
        P(None, "tensor"),
        P(None, "tensor"),
        P("tensor", None),
    )
    out_specs = P("tensor", "dp", None)
    return jax.shard_map(body, mesh=mesh, in_specs=in_specs, out_specs=out_specs, check_vma=False)
```

profile of v0, /device:TPU:0, one launch (start us, length us, event | category | flops | bytes accessed | tf_op | source)
XLA Modules:
  0.0 989.5 jit_solution(14469577349076108792)
XLA Ops:
  39.6 19.7 %all-gather.5.cloned.1.call-done = bf16[512,2,1536]{2,0,1:T(8,128)(2,1)} async-done(((bf16[256,2,1536]{2,0,1:T(8,128)(2,1)}), bf16[512,2,1536]{2,0,1:T(8,128)(2,1)}) %all-gather.5.cloned.1.call-update) | async-done | bytes 3145744 | tf_op jit(solution)/shard_map/all_gather | solution.py:121
  110.2 12.3 %fusion.57 = f32[2,4,2,512,96]{3,4,2,1,0:T(8,128)} fusion(bf16[2,512,4,96,1]{1,3,4,2,0:T(8,128)(2,1)} %bitcast.209, f32[2,4,512,512,2]{3,2,4,1,0:T(8,128)} %get-tuple-element.240, f32[2,4,2,512]{3,2,1,0:T(2,128)S(1)} %broadcast_maximum_fusion, pred[512,512]{0,1:T(8,128)(4,1)S(1)} %copy-done.7, f32[2,4,2,512]{3,2,1,0:T(2,128)S(1)} %get-tuple-element.233), kind=kOutput, calls=%fused_computation.85 | convolution fusion | flops 822870016 | bytes 21037056 | tf_op jit(solution)/shard_map/rhgik,rkhd->rhgid/dot_general | solution.py:54
  122.5 290.3 %while.32 = (s32[]{:T(128)}, f32[2,4,2,512]{3,2,1,0:T(2,128)S(1)}, f32[2,4,2,512]{3,2,1,0:T(2,128)S(1)}, f32[2,4,2,512,96]{3,4,2,1,0:T(8,128)}, s32[8]{0:T(128)S...) while((s32[]{:T(128)}, f32[2,4,2,512]{3,2,1,0:T(2,128)S(1)}, ...), condition=%wide.region_6.7_spmd.clone.clone, body=%wide.region_3.6_spmd.clone.clone.sunk | while | flops 1659127296 | bytes 62922972 | solution.py:181
  135.1 10.3 %fusion.102 = (f32[2,4,2,512]{3,2,1,0:T(2,128)S(1)}, f32[2,4,512,512,2]{3,2,4,1,0:T(8,128)}) fusion(pred[2,512,512]{1,2,0:T(8,128)(4,1)S(1)} %broadcast_and_fusion.2, bf16[512,2,4,2,96]{0,4,3,2,1:T(8,128)(2,1)} %get-tuple-element.408, bf16[2,4096,4,96]{1,3,2,0:T(8,128)(2,1)} %get-tuple-element.407, s32[]{:T(128)S(6)} %select_n.88), kind=kOutput, calls=%fused_computation.33.clone.1 | convolution fusion | flops 817881088 | bytes 19693572 | tf_op jit(solution)/shard_map/while/body/eval_jaxpr/irhgd,rkhd->rhgik/dot_general | solution.py:47
  145.4 9.7 fusion.103
  155.1 13.4 %multiply_add_fusion.11 = f32[2,4,2,512,96]{3,4,2,1,0:T(8,128)} fusion(f32[2,4,2,512,96]{3,4,2,1,0:T(8,128)} %get-tuple-element.391, f32[2,4,512,512,2]{3,2,4,1,0:T(8,128)} %get-tuple-element.372, f32[2,4,2,512]{3,2,1,0:T(2,128)S(1)} %max.12, pred[2,512,512]{1,2,0:T(8,128)(4,1)S(1)} %broadcast_and_fusion.2, f32[2,4,2,512]{3,2,1,0:T(2,128)S(1)} %bitcast.207, ...), kind=kOutput, calls=%fused_computation.36.clone.1 | convolution fusion | flops 823656448 | bytes 24444932 | tf_op jit(solution)/shard_map/while/body/eval_jaxpr/rhgik,rkhd->rhgid/dot_general | solution.py:54
  170.4 10.3 %fusion.102 = (f32[2,4,2,512]{3,2,1,0:T(2,128)S(1)}, f32[2,4,512,512,2]{3,2,4,1,0:T(8,128)}) fusion(pred[2,512,512]{1,2,0:T(8,128)(4,1)S(1)} %broadcast_and_fusion.2, bf16[512,2,4,2,96]{0,4,3,2,1:T(8,128)(2,1)} %get-tuple-element.408, bf16[2,4096,4,96]{1,3,2,0:T(8,128)(2,1)} %get-tuple-element.407, s32[]{:T(128)S(6)} %select_n.88), kind=kOutput, calls=%fused_computation.33.clone.1 | convolution fusion | flops 817881088 | bytes 19693572 | tf_op jit(solution)/shard_map/while/body/eval_jaxpr/irhgd,rkhd->rhgik/dot_general | solution.py:47
  190.1 13.1 %multiply_add_fusion.11 = f32[2,4,2,512,96]{3,4,2,1,0:T(8,128)} fusion(f32[2,4,2,512,96]{3,4,2,1,0:T(8,128)} %get-tuple-element.391, f32[2,4,512,512,2]{3,2,4,1,0:T(8,128)} %get-tuple-element.372, f32[2,4,2,512]{3,2,1,0:T(2,128)S(1)} %max.12, pred[2,512,512]{1,2,0:T(8,128)(4,1)S(1)} %broadcast_and_fusion.2, f32[2,4,2,512]{3,2,1,0:T(2,128)S(1)} %bitcast.207, ...), kind=kOutput, calls=%fused_computation.36.clone.1 | convolution fusion | flops 823656448 | bytes 24444932 | tf_op jit(solution)/shard_map/while/body/eval_jaxpr/rhgik,rkhd->rhgid/dot_general | solution.py:54
  205.1 10.4 %fusion.102 = (f32[2,4,2,512]{3,2,1,0:T(2,128)S(1)}, f32[2,4,512,512,2]{3,2,4,1,0:T(8,128)}) fusion(pred[2,512,512]{1,2,0:T(8,128)(4,1)S(1)} %broadcast_and_fusion.2, bf16[512,2,4,2,96]{0,4,3,2,1:T(8,128)(2,1)} %get-tuple-element.408, bf16[2,4096,4,96]{1,3,2,0:T(8,128)(2,1)} %get-tuple-element.407, s32[]{:T(128)S(6)} %select_n.88), kind=kOutput, calls=%fused_computation.33.clone.1 | convolution fusion | flops 817881088 | bytes 19693572 | tf_op jit(solution)/shard_map/while/body/eval_jaxpr/irhgd,rkhd->rhgik/dot_general | solution.py:47
  215.5 9.5 fusion.103
  225.0 13.6 %multiply_add_fusion.11 = f32[2,4,2,512,96]{3,4,2,1,0:T(8,128)} fusion(f32[2,4,2,512,96]{3,4,2,1,0:T(8,128)} %get-tuple-element.391, f32[2,4,512,512,2]{3,2,4,1,0:T(8,128)} %get-tuple-element.372, f32[2,4,2,512]{3,2,1,0:T(2,128)S(1)} %max.12, pred[2,512,512]{1,2,0:T(8,128)(4,1)S(1)} %broadcast_and_fusion.2, f32[2,4,2,512]{3,2,1,0:T(2,128)S(1)} %bitcast.207, ...), kind=kOutput, calls=%fused_computation.36.clone.1 | convolution fusion | flops 823656448 | bytes 24444932 | tf_op jit(solution)/shard_map/while/body/eval_jaxpr/rhgik,rkhd->rhgid/dot_general | solution.py:54
  240.5 10.3 %fusion.102 = (f32[2,4,2,512]{3,2,1,0:T(2,128)S(1)}, f32[2,4,512,512,2]{3,2,4,1,0:T(8,128)}) fusion(pred[2,512,512]{1,2,0:T(8,128)(4,1)S(1)} %broadcast_and_fusion.2, bf16[512,2,4,2,96]{0,4,3,2,1:T(8,128)(2,1)} %get-tuple-element.408, bf16[2,4096,4,96]{1,3,2,0:T(8,128)(2,1)} %get-tuple-element.407, s32[]{:T(128)S(6)} %select_n.88), kind=kOutput, calls=%fused_computation.33.clone.1 | convolution fusion | flops 817881088 | bytes 19693572 | tf_op jit(solution)/shard_map/while/body/eval_jaxpr/irhgd,rkhd->rhgik/dot_general | solution.py:47
  250.8 9.7 fusion.103
  260.5 13.4 %multiply_add_fusion.11 = f32[2,4,2,512,96]{3,4,2,1,0:T(8,128)} fusion(f32[2,4,2,512,96]{3,4,2,1,0:T(8,128)} %get-tuple-element.391, f32[2,4,512,512,2]{3,2,4,1,0:T(8,128)} %get-tuple-element.372, f32[2,4,2,512]{3,2,1,0:T(2,128)S(1)} %max.12, pred[2,512,512]{1,2,0:T(8,128)(4,1)S(1)} %broadcast_and_fusion.2, f32[2,4,2,512]{3,2,1,0:T(2,128)S(1)} %bitcast.207, ...), kind=kOutput, calls=%fused_computation.36.clone.1 | convolution fusion | flops 823656448 | bytes 24444932 | tf_op jit(solution)/shard_map/while/body/eval_jaxpr/rhgik,rkhd->rhgid/dot_general | solution.py:54
  275.8 10.6 %fusion.102 = (f32[2,4,2,512]{3,2,1,0:T(2,128)S(1)}, f32[2,4,512,512,2]{3,2,4,1,0:T(8,128)}) fusion(pred[2,512,512]{1,2,0:T(8,128)(4,1)S(1)} %broadcast_and_fusion.2, bf16[512,2,4,2,96]{0,4,3,2,1:T(8,128)(2,1)} %get-tuple-element.408, bf16[2,4096,4,96]{1,3,2,0:T(8,128)(2,1)} %get-tuple-element.407, s32[]{:T(128)S(6)} %select_n.88), kind=kOutput, calls=%fused_computation.33.clone.1 | convolution fusion | flops 817881088 | bytes 19693572 | tf_op jit(solution)/shard_map/while/body/eval_jaxpr/irhgd,rkhd->rhgik/dot_general | solution.py:47
  286.4 9.5 fusion.103
  296.0 13.5 %multiply_add_fusion.11 = f32[2,4,2,512,96]{3,4,2,1,0:T(8,128)} fusion(f32[2,4,2,512,96]{3,4,2,1,0:T(8,128)} %get-tuple-element.391, f32[2,4,512,512,2]{3,2,4,1,0:T(8,128)} %get-tuple-element.372, f32[2,4,2,512]{3,2,1,0:T(2,128)S(1)} %max.12, pred[2,512,512]{1,2,0:T(8,128)(4,1)S(1)} %broadcast_and_fusion.2, f32[2,4,2,512]{3,2,1,0:T(2,128)S(1)} %bitcast.207, ...), kind=kOutput, calls=%fused_computation.36.clone.1 | convolution fusion | flops 823656448 | bytes 24444932 | tf_op jit(solution)/shard_map/while/body/eval_jaxpr/rhgik,rkhd->rhgid/dot_general | solution.py:54
  311.4 10.2 %fusion.102 = (f32[2,4,2,512]{3,2,1,0:T(2,128)S(1)}, f32[2,4,512,512,2]{3,2,4,1,0:T(8,128)}) fusion(pred[2,512,512]{1,2,0:T(8,128)(4,1)S(1)} %broadcast_and_fusion.2, bf16[512,2,4,2,96]{0,4,3,2,1:T(8,128)(2,1)} %get-tuple-element.408, bf16[2,4096,4,96]{1,3,2,0:T(8,128)(2,1)} %get-tuple-element.407, s32[]{:T(128)S(6)} %select_n.88), kind=kOutput, calls=%fused_computation.33.clone.1 | convolution fusion | flops 817881088 | bytes 19693572 | tf_op jit(solution)/shard_map/while/body/eval_jaxpr/irhgd,rkhd->rhgik/dot_general | solution.py:47
  330.9 13.1 %multiply_add_fusion.11 = f32[2,4,2,512,96]{3,4,2,1,0:T(8,128)} fusion(f32[2,4,2,512,96]{3,4,2,1,0:T(8,128)} %get-tuple-element.391, f32[2,4,512,512,2]{3,2,4,1,0:T(8,128)} %get-tuple-element.372, f32[2,4,2,512]{3,2,1,0:T(2,128)S(1)} %max.12, pred[2,512,512]{1,2,0:T(8,128)(4,1)S(1)} %broadcast_and_fusion.2, f32[2,4,2,512]{3,2,1,0:T(2,128)S(1)} %bitcast.207, ...), kind=kOutput, calls=%fused_computation.36.clone.1 | convolution fusion | flops 823656448 | bytes 24444932 | tf_op jit(solution)/shard_map/while/body/eval_jaxpr/rhgik,rkhd->rhgid/dot_general | solution.py:54
  345.8 10.2 %fusion.102 = (f32[2,4,2,512]{3,2,1,0:T(2,128)S(1)}, f32[2,4,512,512,2]{3,2,4,1,0:T(8,128)}) fusion(pred[2,512,512]{1,2,0:T(8,128)(4,1)S(1)} %broadcast_and_fusion.2, bf16[512,2,4,2,96]{0,4,3,2,1:T(8,128)(2,1)} %get-tuple-element.408, bf16[2,4096,4,96]{1,3,2,0:T(8,128)(2,1)} %get-tuple-element.407, s32[]{:T(128)S(6)} %select_n.88), kind=kOutput, calls=%fused_computation.33.clone.1 | convolution fusion | flops 817881088 | bytes 19693572 | tf_op jit(solution)/shard_map/while/body/eval_jaxpr/irhgd,rkhd->rhgik/dot_general | solution.py:47
  365.3 13.1 %multiply_add_fusion.11 = f32[2,4,2,512,96]{3,4,2,1,0:T(8,128)} fusion(f32[2,4,2,512,96]{3,4,2,1,0:T(8,128)} %get-tuple-element.391, f32[2,4,512,512,2]{3,2,4,1,0:T(8,128)} %get-tuple-element.372, f32[2,4,2,512]{3,2,1,0:T(2,128)S(1)} %max.12, pred[2,512,512]{1,2,0:T(8,128)(4,1)S(1)} %broadcast_and_fusion.2, f32[2,4,2,512]{3,2,1,0:T(2,128)S(1)} %bitcast.207, ...), kind=kOutput, calls=%fused_computation.36.clone.1 | convolution fusion | flops 823656448 | bytes 24444932 | tf_op jit(solution)/shard_map/while/body/eval_jaxpr/rhgik,rkhd->rhgid/dot_general | solution.py:54
  380.3 10.2 %fusion.102 = (f32[2,4,2,512]{3,2,1,0:T(2,128)S(1)}, f32[2,4,512,512,2]{3,2,4,1,0:T(8,128)}) fusion(pred[2,512,512]{1,2,0:T(8,128)(4,1)S(1)} %broadcast_and_fusion.2, bf16[512,2,4,2,96]{0,4,3,2,1:T(8,128)(2,1)} %get-tuple-element.408, bf16[2,4096,4,96]{1,3,2,0:T(8,128)(2,1)} %get-tuple-element.407, s32[]{:T(128)S(6)} %select_n.88), kind=kOutput, calls=%fused_computation.33.clone.1 | convolution fusion | flops 817881088 | bytes 19693572 | tf_op jit(solution)/shard_map/while/body/eval_jaxpr/irhgd,rkhd->rhgik/dot_general | solution.py:47
  399.8 13.1 %multiply_add_fusion.11 = f32[2,4,2,512,96]{3,4,2,1,0:T(8,128)} fusion(f32[2,4,2,512,96]{3,4,2,1,0:T(8,128)} %get-tuple-element.391, f32[2,4,512,512,2]{3,2,4,1,0:T(8,128)} %get-tuple-element.372, f32[2,4,2,512]{3,2,1,0:T(2,128)S(1)} %max.12, pred[2,512,512]{1,2,0:T(8,128)(4,1)S(1)} %broadcast_and_fusion.2, f32[2,4,2,512]{3,2,1,0:T(2,128)S(1)} %bitcast.207, ...), kind=kOutput, calls=%fused_computation.36.clone.1 | convolution fusion | flops 823656448 | bytes 24444932 | tf_op jit(solution)/shard_map/while/body/eval_jaxpr/rhgik,rkhd->rhgid/dot_general | solution.py:54
  412.9 17.3 %fusion.68 = (bf16[8,2048,384]{2,1,0:T(8,128)(2,1)}, bf16[8,2048,384]{2,1,0:T(8,128)(2,1)}) fusion(bf16[8,4096,384]{2,1,0:T(8,128)(2,1)} %all-gather.7.cloned.1.call-done), kind=kLoop, calls=%fused_computation.114 | loop fusion | bytes 50331648 | tf_op jit(solution)/shard_map/jit(_take)/gather | solution.py:72
  444.6 17.1 %fusion.67 = (bf16[8,2048,384]{2,1,0:T(8,128)(2,1)}, bf16[8,2048,384]{2,1,0:T(8,128)(2,1)}) fusion(bf16[8,4096,384]{2,1,0:T(8,128)(2,1)} %all-gather.9.cloned.1.call-done), kind=kLoop, calls=%fused_computation.113 | loop fusion | bytes 50331648 | tf_op jit(solution)/shard_map/jit(_take)/gather | solution.py:75
  476.2 11.4 %maximum_select_fusion.1 = (bf16[2,4096,384]{2,1,0:T(8,128)(2,1)}, bf16[2,4096,384]{2,1,0:T(8,128)(2,1)}) fusion(bf16[2,2048,384]{2,1,0:T(8,128)(2,1)} %gather_fusion.3, bf16[2,2048,384]{2,1,0:T(8,128)(2,1)} %gather_fusion.2, pred[2]{0:T(512)(128)(4,1)S(1)} %copy-done.12, bf16[2,2048,384]{2,1,0:T(8,128)(2,1)} %gather_fusion.1, ...), kind=kLoop, calls=%fused_computation.62 | loop fusion | flops 31457280 | bytes 25165826 | tf_op jit(solution)/shard_map/jit(_take)/select_n | solution.py:75
  504.9 275.1 %while.31 = (s32[]{:T(128)}, f32[2,4,2,512]{3,2,1,0:T(2,128)S(1)}, f32[2,4,2,512]{3,2,1,0:T(2,128)S(1)}, f32[2,4,2,512,96]{3,4,2,1,0:T(8,128)}, s32[8]{0:T(128)S...) while((s32[]{:T(128)}, f32[2,4,2,512]{3,2,1,0:T(2,128)S(1)}, ...), condition=%wide.region_10.12_spmd.clone, body=%wide.region_7.0_spmd.clone.sunk | while | flops 1659391488 | bytes 62403788 | solution.py:90
  507.0 10.2 %fusion.97 = (f32[2,4,2,512]{3,2,1,0:T(2,128)S(1)}, f32[2,4,512,512,2]{3,2,4,1,0:T(8,128)}) fusion(pred[2,512,512]{1,2,0:T(8,128)(4,1)S(1)} %compare_or_fusion.2, bf16[512,2,4,2,96]{0,4,3,2,1:T(8,128)(2,1)} %get-tuple-element.446, bf16[2,4096,4,96]{1,3,2,0:T(8,128)(2,1)} %get-tuple-element.445, s32[]{:T(128)S(6)} %select_n.84), kind=kOutput, calls=%fused_computation.10.clone.1 | convolution fusion | flops 817881088 | bytes 19693572 | tf_op jit(solution)/shard_map/while/body/eval_jaxpr/irhgd,rkhd->rhgik/dot_general | solution.py:47
  526.5 13.1 %multiply_add_fusion.9 = f32[2,4,2,512,96]{3,4,2,1,0:T(8,128)} fusion(f32[2,4,2,512,96]{3,4,2,1,0:T(8,128)} %get-tuple-element.430, f32[2,4,512,512,2]{3,2,4,1,0:T(8,128)} %get-tuple-element.359, f32[2,4,2,512]{3,2,1,0:T(2,128)S(1)} %max.11, pred[2,512,512]{1,2,0:T(8,128)(4,1)S(1)} %compare_or_fusion.2, f32[2,4,2,512]{3,2,1,0:T(2,128)S(1)} %bitcast.208, ...), kind=kOutput, calls=%fused_computation.13.clone.1 | convolution fusion | flops 823656448 | bytes 24444932 | tf_op jit(solution)/shard_map/while/body/eval_jaxpr/rhgik,rkhd->rhgid/dot_general | solution.py:54
  541.4 10.2 %fusion.97 = (f32[2,4,2,512]{3,2,1,0:T(2,128)S(1)}, f32[2,4,512,512,2]{3,2,4,1,0:T(8,128)}) fusion(pred[2,512,512]{1,2,0:T(8,128)(4,1)S(1)} %compare_or_fusion.2, bf16[512,2,4,2,96]{0,4,3,2,1:T(8,128)(2,1)} %get-tuple-element.446, bf16[2,4096,4,96]{1,3,2,0:T(8,128)(2,1)} %get-tuple-element.445, s32[]{:T(128)S(6)} %select_n.84), kind=kOutput, calls=%fused_computation.10.clone.1 | convolution fusion | flops 817881088 | bytes 19693572 | tf_op jit(solution)/shard_map/while/body/eval_jaxpr/irhgd,rkhd->rhgik/dot_general | solution.py:47
  560.9 13.1 %multiply_add_fusion.9 = f32[2,4,2,512,96]{3,4,2,1,0:T(8,128)} fusion(f32[2,4,2,512,96]{3,4,2,1,0:T(8,128)} %get-tuple-element.430, f32[2,4,512,512,2]{3,2,4,1,0:T(8,128)} %get-tuple-element.359, f32[2,4,2,512]{3,2,1,0:T(2,128)S(1)} %max.11, pred[2,512,512]{1,2,0:T(8,128)(4,1)S(1)} %compare_or_fusion.2, f32[2,4,2,512]{3,2,1,0:T(2,128)S(1)} %bitcast.208, ...), kind=kOutput, calls=%fused_computation.13.clone.1 | convolution fusion | flops 823656448 | bytes 24444932 | tf_op jit(solution)/shard_map/while/body/eval_jaxpr/rhgik,rkhd->rhgid/dot_general | solution.py:54
  575.7 10.2 %fusion.97 = (f32[2,4,2,512]{3,2,1,0:T(2,128)S(1)}, f32[2,4,512,512,2]{3,2,4,1,0:T(8,128)}) fusion(pred[2,512,512]{1,2,0:T(8,128)(4,1)S(1)} %compare_or_fusion.2, bf16[512,2,4,2,96]{0,4,3,2,1:T(8,128)(2,1)} %get-tuple-element.446, bf16[2,4096,4,96]{1,3,2,0:T(8,128)(2,1)} %get-tuple-element.445, s32[]{:T(128)S(6)} %select_n.84), kind=kOutput, calls=%fused_computation.10.clone.1 | convolution fusion | flops 817881088 | bytes 19693572 | tf_op jit(solution)/shard_map/while/body/eval_jaxpr/irhgd,rkhd->rhgik/dot_general | solution.py:47
  595.2 13.1 %multiply_add_fusion.9 = f32[2,4,2,512,96]{3,4,2,1,0:T(8,128)} fusion(f32[2,4,2,512,96]{3,4,2,1,0:T(8,128)} %get-tuple-element.430, f32[2,4,512,512,2]{3,2,4,1,0:T(8,128)} %get-tuple-element.359, f32[2,4,2,512]{3,2,1,0:T(2,128)S(1)} %max.11, pred[2,512,512]{1,2,0:T(8,128)(4,1)S(1)} %compare_or_fusion.2, f32[2,4,2,512]{3,2,1,0:T(2,128)S(1)} %bitcast.208, ...), kind=kOutput, calls=%fused_computation.13.clone.1 | convolution fusion | flops 823656448 | bytes 24444932 | tf_op jit(solution)/shard_map/while/body/eval_jaxpr/rhgik,rkhd->rhgid/dot_general | solution.py:54
  610.0 10.2 %fusion.97 = (f32[2,4,2,512]{3,2,1,0:T(2,128)S(1)}, f32[2,4,512,512,2]{3,2,4,1,0:T(8,128)}) fusion(pred[2,512,512]{1,2,0:T(8,128)(4,1)S(1)} %compare_or_fusion.2, bf16[512,2,4,2,96]{0,4,3,2,1:T(8,128)(2,1)} %get-tuple-element.446, bf16[2,4096,4,96]{1,3,2,0:T(8,128)(2,1)} %get-tuple-element.445, s32[]{:T(128)S(6)} %select_n.84), kind=kOutput, calls=%fused_computation.10.clone.1 | convolution fusion | flops 817881088 | bytes 19693572 | tf_op jit(solution)/shard_map/while/body/eval_jaxpr/irhgd,rkhd->rhgik/dot_general | solution.py:47
  629.5 13.1 %multiply_add_fusion.9 = f32[2,4,2,512,96]{3,4,2,1,0:T(8,128)} fusion(f32[2,4,2,512,96]{3,4,2,1,0:T(8,128)} %get-tuple-element.430, f32[2,4,512,512,2]{3,2,4,1,0:T(8,128)} %get-tuple-element.359, f32[2,4,2,512]{3,2,1,0:T(2,128)S(1)} %max.11, pred[2,512,512]{1,2,0:T(8,128)(4,1)S(1)} %compare_or_fusion.2, f32[2,4,2,512]{3,2,1,0:T(2,128)S(1)} %bitcast.208, ...), kind=kOutput, calls=%fused_computation.13.clone.1 | convolution fusion | flops 823656448 | bytes 24444932 | tf_op jit(solution)/shard_map/while/body/eval_jaxpr/rhgik,rkhd->rhgid/dot_general | solution.py:54
  644.4 10.2 %fusion.97 = (f32[2,4,2,512]{3,2,1,0:T(2,128)S(1)}, f32[2,4,512,512,2]{3,2,4,1,0:T(8,128)}) fusion(pred[2,512,512]{1,2,0:T(8,128)(4,1)S(1)} %compare_or_fusion.2, bf16[512,2,4,2,96]{0,4,3,2,1:T(8,128)(2,1)} %get-tuple-element.446, bf16[2,4096,4,96]{1,3,2,0:T(8,128)(2,1)} %get-tuple-element.445, s32[]{:T(128)S(6)} %select_n.84), kind=kOutput, calls=%fused_computation.10.clone.1 | convolution fusion | flops 817881088 | bytes 19693572 | tf_op jit(solution)/shard_map/while/body/eval_jaxpr/irhgd,rkhd->rhgik/dot_general | solution.py:47
  663.9 13.1 %multiply_add_fusion.9 = f32[2,4,2,512,96]{3,4,2,1,0:T(8,128)} fusion(f32[2,4,2,512,96]{3,4,2,1,0:T(8,128)} %get-tuple-element.430, f32[2,4,512,512,2]{3,2,4,1,0:T(8,128)} %get-tuple-element.359, f32[2,4,2,512]{3,2,1,0:T(2,128)S(1)} %max.11, pred[2,512,512]{1,2,0:T(8,128)(4,1)S(1)} %compare_or_fusion.2, f32[2,4,2,512]{3,2,1,0:T(2,128)S(1)} %bitcast.208, ...), kind=kOutput, calls=%fused_computation.13.clone.1 | convolution fusion | flops 823656448 | bytes 24444932 | tf_op jit(solution)/shard_map/while/body/eval_jaxpr/rhgik,rkhd->rhgid/dot_general | solution.py:54
  678.7 10.2 %fusion.97 = (f32[2,4,2,512]{3,2,1,0:T(2,128)S(1)}, f32[2,4,512,512,2]{3,2,4,1,0:T(8,128)}) fusion(pred[2,512,512]{1,2,0:T(8,128)(4,1)S(1)} %compare_or_fusion.2, bf16[512,2,4,2,96]{0,4,3,2,1:T(8,128)(2,1)} %get-tuple-element.446, bf16[2,4096,4,96]{1,3,2,0:T(8,128)(2,1)} %get-tuple-element.445, s32[]{:T(128)S(6)} %select_n.84), kind=kOutput, calls=%fused_computation.10.clone.1 | convolution fusion | flops 817881088 | bytes 19693572 | tf_op jit(solution)/shard_map/while/body/eval_jaxpr/irhgd,rkhd->rhgik/dot_general | solution.py:47
  698.2 13.1 %multiply_add_fusion.9 = f32[2,4,2,512,96]{3,4,2,1,0:T(8,128)} fusion(f32[2,4,2,512,96]{3,4,2,1,0:T(8,128)} %get-tuple-element.430, f32[2,4,512,512,2]{3,2,4,1,0:T(8,128)} %get-tuple-element.359, f32[2,4,2,512]{3,2,1,0:T(2,128)S(1)} %max.11, pred[2,512,512]{1,2,0:T(8,128)(4,1)S(1)} %compare_or_fusion.2, f32[2,4,2,512]{3,2,1,0:T(2,128)S(1)} %bitcast.208, ...), kind=kOutput, calls=%fused_computation.13.clone.1 | convolution fusion | flops 823656448 | bytes 24444932 | tf_op jit(solution)/shard_map/while/body/eval_jaxpr/rhgik,rkhd->rhgid/dot_general | solution.py:54
  713.1 10.2 %fusion.97 = (f32[2,4,2,512]{3,2,1,0:T(2,128)S(1)}, f32[2,4,512,512,2]{3,2,4,1,0:T(8,128)}) fusion(pred[2,512,512]{1,2,0:T(8,128)(4,1)S(1)} %compare_or_fusion.2, bf16[512,2,4,2,96]{0,4,3,2,1:T(8,128)(2,1)} %get-tuple-element.446, bf16[2,4096,4,96]{1,3,2,0:T(8,128)(2,1)} %get-tuple-element.445, s32[]{:T(128)S(6)} %select_n.84), kind=kOutput, calls=%fused_computation.10.clone.1 | convolution fusion | flops 817881088 | bytes 19693572 | tf_op jit(solution)/shard_map/while/body/eval_jaxpr/irhgd,rkhd->rhgik/dot_general | solution.py:47
  732.6 13.1 %multiply_add_fusion.9 = f32[2,4,2,512,96]{3,4,2,1,0:T(8,128)} fusion(f32[2,4,2,512,96]{3,4,2,1,0:T(8,128)} %get-tuple-element.430, f32[2,4,512,512,2]{3,2,4,1,0:T(8,128)} %get-tuple-element.359, f32[2,4,2,512]{3,2,1,0:T(2,128)S(1)} %max.11, pred[2,512,512]{1,2,0:T(8,128)(4,1)S(1)} %compare_or_fusion.2, f32[2,4,2,512]{3,2,1,0:T(2,128)S(1)} %bitcast.208, ...), kind=kOutput, calls=%fused_computation.13.clone.1 | convolution fusion | flops 823656448 | bytes 24444932 | tf_op jit(solution)/shard_map/while/body/eval_jaxpr/rhgik,rkhd->rhgid/dot_general | solution.py:54
  747.4 10.2 %fusion.97 = (f32[2,4,2,512]{3,2,1,0:T(2,128)S(1)}, f32[2,4,512,512,2]{3,2,4,1,0:T(8,128)}) fusion(pred[2,512,512]{1,2,0:T(8,128)(4,1)S(1)} %compare_or_fusion.2, bf16[512,2,4,2,96]{0,4,3,2,1:T(8,128)(2,1)} %get-tuple-element.446, bf16[2,4096,4,96]{1,3,2,0:T(8,128)(2,1)} %get-tuple-element.445, s32[]{:T(128)S(6)} %select_n.84), kind=kOutput, calls=%fused_computation.10.clone.1 | convolution fusion | flops 817881088 | bytes 19693572 | tf_op jit(solution)/shard_map/while/body/eval_jaxpr/irhgd,rkhd->rhgik/dot_general | solution.py:47
  766.9 13.1 %multiply_add_fusion.9 = f32[2,4,2,512,96]{3,4,2,1,0:T(8,128)} fusion(f32[2,4,2,512,96]{3,4,2,1,0:T(8,128)} %get-tuple-element.430, f32[2,4,512,512,2]{3,2,4,1,0:T(8,128)} %get-tuple-element.359, f32[2,4,2,512]{3,2,1,0:T(2,128)S(1)} %max.11, pred[2,512,512]{1,2,0:T(8,128)(4,1)S(1)} %compare_or_fusion.2, f32[2,4,2,512]{3,2,1,0:T(2,128)S(1)} %bitcast.208, ...), kind=kOutput, calls=%fused_computation.13.clone.1 | convolution fusion | flops 823656448 | bytes 24444932 | tf_op jit(solution)/shard_map/while/body/eval_jaxpr/rhgik,rkhd->rhgid/dot_general | solution.py:54
  786.8 43.5 %reduce-scatter.3.cloned.1.call-done = bf16[256,2,1536]{2,0,1:T(8,128)(2,1)} async-done(((bf16[512,2,1536]{2,0,1:T(8,128)(2,1)}), bf16[256,2,1536]{2,0,1:T(8,128)(2,1)}) %reduce-scatter.3.cloned.1.call-update) | async-done | bytes 1572880 | tf_op jit(solution)/shard_map/reduce_scatter | solution.py:200
  834.7 45.0 %all-gather.11.cloned.1.call-done = bf16[512,2,1536]{2,0,1:T(8,128)(2,1)} async-done(((bf16[256,2,1536]{2,0,1:T(8,128)(2,1)}), bf16[512,2,1536]{2,0,1:T(8,128)(2,1)}) %all-gather.11.cloned.1.call-update) | async-done | bytes 3145744 | tf_op jit(solution)/shard_map/all_gather | solution.py:213
  894.1 9.8 fusion.69
  903.9 9.6 multiply_convert_fusion
  933.2 43.5 %reduce-scatter.5.cloned.1.call-done = bf16[256,2,1536]{2,0,1:T(8,128)(2,1)} async-done(((bf16[512,2,1536]{2,0,1:T(8,128)(2,1)}), bf16[256,2,1536]{2,0,1:T(8,128)(2,1)}) %reduce-scatter.5.cloned.1.call-update) | async-done | bytes 1572880 | tf_op jit(solution)/shard_map/reduce_scatter | solution.py:224
  (246 shorter events, 311.2 us)
Async XLA Ops:
  6.5 775.8 %copy-start = (bf16[768,1536]{1,0:T(8,128)(2,1)S(1)}, bf16[768,1536]{1,0:T(8,128)(2,1)}, u32[]{:S(2)}) copy-start(bf16[768,1536]{1,0:T(8,128)(2,1)} %param.29) | copy-start | bytes 7077892
  6.5 52.8 %all-gather.5.cloned.1.call-start = ((), (), s32[]{:S(2)}) async-start(), calls=%async_computation.2 | async-start | bytes 4718592 | tf_op jit(solution)/shard_map/all_gather | solution.py:121
  11.5 401.4 %all-gather.7.cloned.1.call-start = ((), (), s32[]{:S(2)}) async-start(), calls=%async_computation.3 | async-start | bytes 26738688 | tf_op jit(solution)/shard_map/all_gather | solution.py:188
  12.3 5.1 copy-start.5
  12.3 432.3 %all-gather.9.cloned.1.call-start = ((), (), s32[]{:S(2)}) async-start(), calls=%async_computation.4 | async-start | bytes 26738688 | tf_op jit(solution)/shard_map/all_gather | solution.py:189
  13.0 817.2 %reduce-scatter.3.cloned.1.call-start = ((), (), s32[]{:S(2)}) async-start(), calls=%async_computation.5 | async-start | bytes 4718592 | tf_op jit(solution)/shard_map/reduce_scatter | solution.py:200
  27.7 8.7 copy-start.13
  27.7 10.6 %copy-start.14 = (s32[2]{0:T(128)S(1)}, s32[2]{0:T(128)}, u32[]{:S(2)}) copy-start(s32[2]{0:T(128)} %param.23) | copy-start | bytes 28
  38.3 0.5 copy-start.8
  88.6 2.5 copy-start.3
  88.6 2.8 copy-start.6
  91.4 1.7 copy-start.7
  412.9 17.3 %copy-start.10 = (s32[1024]{0:T(1024)S(1)}, s32[1024]{0:T(1024)}, u32[]{:S(2)}) copy-start(s32[1024]{0:T(1024)} %pad_clamp_fusion) | copy-start | bytes 12292
  468.9 7.3 copy-start.12
  496.3 8.6 copy-start.9
  786.7 46.1 %copy-start.11 = (f32[1536]{0:T(1024)S(1)}, f32[1536]{0:T(1024)}, u32[]{:S(2)}) copy-start(f32[1536]{0:T(1024)} %param.34) | copy-start | bytes 18436
  786.7 93.1 %all-gather.11.cloned.1.call-start = ((), (), s32[]{:S(2)}) async-start(), calls=%async_computation.6 | async-start | bytes 4718592 | tf_op jit(solution)/shard_map/all_gather | solution.py:213
  830.2 2.5 copy-start.1
  830.2 2.8 copy-start.2
  834.7 142.0 %reduce-scatter.5.cloned.1.call-start = ((), (), s32[]{:S(2)}) async-start(), calls=%async_computation.7 | async-start | bytes 4718592 | tf_op jit(solution)/shard_map/reduce_scatter | solution.py:224
  894.0 9.9 copy-start.4
  894.1 19.5 %slice-start = ((s8[6291456]{0:T(1024)(128)(4,1)}), s8[4194304]{0:T(1024)(128)(4,1)S(1)}, s32[]{:S(2)}) async-start(s8[6291456]{0:T(1024)(128)(4,1)} %bitcast.210), calls=%async_computation.8 | async-start | bytes 8388608
  903.9 9.7 slice-start.1
Sparse Core Ops, SparseCore 0:
  11.6 47.6 all-gather.4
  60.8 128.5 all-gather.6
  191.0 128.5 all-gather.8
  786.8 43.3 reduce-scatter.2
  834.8 44.9 all-gather.10
  933.3 43.3 reduce-scatter.4
where the time goes:
time: 995 us; the launch traced here: 989 us
  matrix products  439 us (44%)
  other arithmetic  199 us (20%)
  local copies, waits for them, and re-layouts  163 us (16%)
  waiting for transfers between devices  153 us (15%)
  loops' own time  21.7 us (2%)
  between operations  14 us (1%)
    dot_general x17, matrix products, absorb(): jnp.einsum('rhgik,rkhd->rhgid', weights.astype(jnp.bfloat16), value_block...  223 us
    dot_general x17, matrix products, absorb(): jnp.einsum('irhgd,rkhd->rhgik', queries, key_block, preferred_element_typ...  172 us
    reduce_sum x17, other arithmetic, absorb(): jnp.sum(weights, axis=-1)  159 us
    reduce_scatter x2, waiting for transfers between devices, body(): lax.psum_scatter(jnp.dot(picked.reshape(lax.axis_size('tensor') * local_r...  87 us
    all_gather x1, waiting for transfers between devices, body(): lax.all_gather(norm_rows(residual, mlp_gain), 'tensor', axis=0, tiled=True)  45 us
    gather x3, local copies, waits for them, and re-layouts, shared_block(): jnp.take(key_piece, selector, axis=0)  31.7 us
    gather x3, local copies, waits for them, and re-layouts, shared_block(): jnp.take(value_piece, selector, axis=0)  31.6 us
    unnamed x38, local copies, waits for them, and re-layouts  25.1 us
  transfers between devices with their start and end apart: 6, of which 4 were waited for; matrix products, arithmetic and copies ran while one was open for 40% of the time, Pallas kernels for 0%

commit v1 on v0

v1 whole, which is shorter than its diff:
```python
import functools
import math

import jax
import jax.numpy as jnp
from jax import lax
from jax.experimental import pallas as pl
from jax.experimental.pallas import tpu as pltpu
from jax.sharding import PartitionSpec as P

MODEL_WIDTH = 1536
HEAD_SIZE = 96
FRESH_TOKENS = 512
WINDOW_SPAN = 4096
SINKS = 4
PROMPT_TOKENS = 4096

rope_base = 10000.0
epsilon = 1e-05
far_below = -1e30
EXP2_SCALE = math.log2(math.e) / math.sqrt(HEAD_SIZE)
QUERY_TILE = 256
CACHE_BLOCK = 256
SUM_ROWS = 16


def norm_rows(values, gain_vec):
    widened = values.astype(jnp.float32)
    factor = lax.rsqrt(jnp.mean(widened * widened, axis=-1, keepdims=True) + epsilon)
    return (widened * factor * gain_vec).astype(jnp.bfloat16)


def rotate_columns(values, positions):
    requests, rows, tokens = values.shape
    half_dim = HEAD_SIZE // 2
    frequency = rope_base ** (-2.0 * jnp.arange(half_dim, dtype=jnp.float32) / HEAD_SIZE)
    angles = positions.astype(jnp.float32)[:, None, None, :] * frequency[None, None, :, None]
    cosine = jnp.cos(angles)
    sine_part = jnp.sin(angles)
    split = values.reshape(requests, rows // HEAD_SIZE, 2, half_dim, tokens)
    first_half = split[:, :, 0]
    second_half = split[:, :, 1]
    turned = jnp.concatenate(
        [
            first_half * cosine - second_half * sine_part,
            second_half * cosine + first_half * sine_part,
        ],
        axis=2,
    )
    return turned.astype(jnp.bfloat16).reshape(requests, rows, tokens)


def attention_kernel(
    group_ref,
    len_ref,
    q_ref,
    fresh_k_ref,
    fresh_v_ref,
    cache_k_ref,
    cache_v_ref,
    prompt_ref,
    out_ref,
    peak_ref,
    sum_ref,
):
    length = len_ref[pl.program_id(0)]
    heads = q_ref.shape[1] // HEAD_SIZE
    halves = FRESH_TOKENS // QUERY_TILE
    piece = prompt_ref.shape[3]
    pieces = prompt_ref.shape[0]
    peak_ref[...] = jnp.full(peak_ref.shape, far_below, jnp.float32)
    sum_ref[...] = jnp.zeros(sum_ref.shape, jnp.float32)

    def absorb(keys, values, visible, tiles=None):
        block = keys.shape[1]
        turned = keys.T
        widened = jnp.concatenate([values, jnp.ones((SUM_ROWS, block), jnp.bfloat16)], axis=0)
        for half in range(halves):
            if tiles is not None and half not in tiles:
                continue
            mask = None
            if visible is not None:
                key_ids = lax.broadcasted_iota(jnp.int32, (block, QUERY_TILE), 0)
                row_ids = lax.broadcasted_iota(jnp.int32, (block, QUERY_TILE), 1)
                mask = visible(key_ids, row_ids + half * QUERY_TILE)
            for head in range(heads):
                place = head * halves + half
                query = q_ref[
                    0,
                    head * HEAD_SIZE : (head + 1) * HEAD_SIZE,
                    half * QUERY_TILE : (half + 1) * QUERY_TILE,
                ]
                scores = jnp.dot(turned, query, preferred_element_type=jnp.float32)
                if mask is not None:
                    scores = jnp.where(mask, scores, far_below)
                old_peak = peak_ref[place : place + 1, :]
                new_peak = jnp.maximum(old_peak, jnp.max(scores, axis=0, keepdims=True))
                peak_ref[place : place + 1, :] = new_peak
                factor = jnp.exp2((old_peak - new_peak) * EXP2_SCALE)
                weights = jnp.exp2((scores - new_peak) * EXP2_SCALE).astype(jnp.bfloat16)
                sum_ref[place] = sum_ref[place] * factor + jnp.dot(
                    widened, weights, preferred_element_type=jnp.float32
                )

    for start in range(0, FRESH_TOKENS, QUERY_TILE):
        absorb(
            fresh_k_ref[0, :, start : start + QUERY_TILE],
            fresh_v_ref[0, :, start : start + QUERY_TILE],
            lambda keys, rows, start=start: keys + start <= rows,
            tiles=range(start // QUERY_TILE, halves),
        )

    def cache_step(masked, index):
        start = pl.multiple_of(index * CACHE_BLOCK, CACHE_BLOCK)
        columns = pl.ds(start, CACHE_BLOCK)
        absorb(
            cache_k_ref[0, :, columns],
            cache_v_ref[0, :, columns],
            (
                lambda keys, rows: (keys + start >= WINDOW_SPAN - length) & (keys + start > rows)
            )
            if masked
            else None,
        )

    cache_blocks = WINDOW_SPAN // CACHE_BLOCK
    first = jnp.maximum((WINDOW_SPAN - length) // CACHE_BLOCK, 0)
    clear = jnp.minimum(jnp.maximum(first + 1, FRESH_TOKENS // CACHE_BLOCK), cache_blocks)

    def prompt_step(masked, index):
        start = index * piece
        absorb(
            prompt_ref[index, 0, 0:HEAD_SIZE, :],
            prompt_ref[index, 0, HEAD_SIZE : 2 * HEAD_SIZE, :],
            (lambda keys, rows: (keys + start < SINKS) | (keys + start > length + rows))
            if masked
            else None,
        )

    def run(low, high, step):
        def body(index, carry):
            step(index)
            return carry

        lax.fori_loop(low, high, body, 0)

    run(first, clear, functools.partial(cache_step, True))
    run(clear, cache_blocks, functools.partial(cache_step, False))
    prompt_step(True, 0)
    begin = jnp.minimum(jnp.maximum((length + 1) // piece, 1), pieces)
    open_from = jnp.clip((length + FRESH_TOKENS - 1) // piece + 1, begin, pieces)
    run(begin, open_from, functools.partial(prompt_step, True))
    run(open_from, pieces, functools.partial(prompt_step, False))

    for head in range(heads):
        for half in range(halves):
            total = sum_ref[head * halves + half]
            out_ref[
                0,
                head * HEAD_SIZE : (head + 1) * HEAD_SIZE,
                half * QUERY_TILE : (half + 1) * QUERY_TILE,
            ] = (total[:HEAD_SIZE] / total[HEAD_SIZE : HEAD_SIZE + 1]).astype(jnp.bfloat16)


def attend(groups, lengths, queries, fresh_k, fresh_v, cache_k, cache_v, prompts, first_head):
    requests = queries.shape[0]
    group_width = queries.shape[1] // cache_k.shape[1]
    heads = prompts.shape[2] // (2 * HEAD_SIZE)
    pieces, piece = prompts.shape[0], prompts.shape[3]
    query_rows = group_width * HEAD_SIZE
    own = lambda r, h, *_: (r, first_head + h, 0)
    places = group_width * FRESH_TOKENS // QUERY_TILE
    scores = requests * heads * group_width * FRESH_TOKENS * (WINDOW_SPAN + FRESH_TOKENS)
    return pl.pallas_call(
        attention_kernel,
        grid_spec=pltpu.PrefetchScalarGridSpec(
            num_scalar_prefetch=2,
            grid=(requests, heads),
            in_specs=[
                pl.BlockSpec((1, query_rows, FRESH_TOKENS), own),
                pl.BlockSpec((1, HEAD_SIZE, FRESH_TOKENS), own),
                pl.BlockSpec((1, HEAD_SIZE, FRESH_TOKENS), own),
                pl.BlockSpec((1, HEAD_SIZE, WINDOW_SPAN), own),
                pl.BlockSpec((1, HEAD_SIZE, WINDOW_SPAN), own),
                pl.BlockSpec(
                    (pieces, 1, 2 * HEAD_SIZE, piece), lambda r, h, group, _: (0, group[r], h, 0)
                ),
            ],
            out_specs=pl.BlockSpec((1, query_rows, FRESH_TOKENS), lambda r, h, *_: (r, h, 0)),
            scratch_shapes=[
                pltpu.VMEM((max(places, 8), QUERY_TILE), jnp.float32),
                pltpu.VMEM((places, HEAD_SIZE + SUM_ROWS, QUERY_TILE), jnp.float32),
            ],
        ),
        out_shape=jax.ShapeDtypeStruct((requests, heads * query_rows, FRESH_TOKENS), jnp.bfloat16),
        compiler_params=pltpu.CompilerParams(
            dimension_semantics=("arbitrary", "arbitrary"), vmem_limit_bytes=40 * 1024 * 1024
        ),
        cost_estimate=pl.CostEstimate(
            flops=4 * 256 * scores,
            bytes_accessed=requests * heads * 4 * HEAD_SIZE * 2 * (WINDOW_SPAN + PROMPT_TOKENS),
            transcendentals=scores,
        ),
        name="attend",
    )(groups, lengths, queries, fresh_k, fresh_v, cache_k, cache_v, prompts)


def body(
    dp_size,
    tensor_size,
    tokens,
    cached_len,
    prompt_group,
    attn_gain,
    w_query,
    key_matrix,
    value_matrix,
    w_out,
    window_cache_keys,
    window_cache_values,
    prompt_keys,
    prompt_values,
    mlp_gain,
    w_gate,
    w_up,
    w_down,
):
    local_rows, local_reqs = tokens.shape[:2]
    query_cols = w_query.shape[1]
    key_cols = key_matrix.shape[1]
    key_heads = key_cols // HEAD_SIZE
    paired = tensor_size == 2 and dp_size % 2 == 0
    swap = [(0, 1), (1, 0)]
    across = [(rank, rank ^ 1) for rank in range(dp_size)]
    tensor_rank = lax.axis_index("tensor")
    core = lax.axis_index("dp") % 2

    chunk_heads = max(key_heads // 2, 1)
    chunks = key_heads // chunk_heads
    group_count, piece = prompt_keys.shape[:2]
    by_head = lambda a: a.transpose(0, 2, 1).reshape(group_count, key_heads, HEAD_SIZE, piece)
    packed = jnp.concatenate([by_head(prompt_keys), by_head(prompt_values)], axis=2)
    prompts = []
    for chunk in range(chunks):
        part = packed[:, chunk * chunk_heads : (chunk + 1) * chunk_heads].reshape(
            group_count, chunk_heads * 2 * HEAD_SIZE, piece
        )
        if prompts:
            part, prompts[-1] = lax.optimization_barrier((part, prompts[-1]))
        prompts.append(lax.all_gather(part, "dp", axis=0))

    source = norm_rows(tokens.transpose(1, 0, 2), attn_gain)
    if paired:
        other = lax.ppermute(source, "tensor", swap)
        low = tensor_rank == 0
        normed = jnp.concatenate(
            [jnp.where(low, source, other), jnp.where(low, other, source)], axis=1
        )
    else:
        normed = lax.all_gather(source, "tensor", axis=1, tiled=True)

    def fetch(weight, axis, after):
        if not paired:
            return [lax.all_gather(weight, "tensor", axis=axis, tiled=True)]
        weight, _ = lax.optimization_barrier((weight, after))
        half = weight.shape[axis] // 2
        sent = lax.dynamic_slice_in_dim(weight, core * half, half, axis)
        mine = lax.ppermute(sent, "tensor", swap)
        return [weight, mine, lax.ppermute(mine, "dp", across)]

    out_parts = fetch(w_out, 0, normed)
    gate_parts = fetch(w_gate, 1, out_parts[-1])
    up_parts = fetch(w_up, 1, gate_parts[-1])
    down_parts = fetch(w_down, 0, up_parts[-1])

    positions = (
        PROMPT_TOKENS + cached_len[:, None] + jnp.arange(FRESH_TOKENS, dtype=jnp.int32)[None, :]
    )

    def project(weight):
        return jnp.stack(
            [
                lax.dot_general(
                    weight,
                    normed[request],
                    (((0,), (1,)), ((), ())),
                    preferred_element_type=jnp.float32,
                )
                for request in range(local_reqs)
            ]
        )

    queries = rotate_columns(project(w_query), positions)
    fresh_keys = rotate_columns(project(key_matrix), positions)
    fresh_values = project(value_matrix).astype(jnp.bfloat16)
    past_keys = window_cache_keys.transpose(0, 2, 1)
    past_values = window_cache_values.transpose(0, 2, 1)

    chunk_cols = query_cols // chunks
    attn_part = jnp.zeros((local_reqs * local_rows, MODEL_WIDTH), jnp.float32)

    def add_out(total, attended, weight):
        return total + jnp.concatenate(
            [
                lax.dot_general(
                    attended[request],
                    weight,
                    (((0,), (0,)), ((), ())),
                    preferred_element_type=jnp.float32,
                )
                for request in range(local_reqs)
            ]
        )

    for chunk in range(chunks):
        attended = attend(
            prompt_group,
            cached_len,
            queries,
            fresh_keys,
            fresh_values,
            past_keys,
            past_values,
            prompts[chunk],
            chunk * chunk_heads,
        )
        if paired:
            mine = lax.dynamic_slice_in_dim(attended, tensor_rank * local_rows, local_rows, 2)
            sent = lax.dynamic_slice_in_dim(attended, (1 - tensor_rank) * local_rows, local_rows, 2)
            got = lax.ppermute(sent, "tensor", swap)
            own_rows = out_parts[0][chunk * chunk_cols : (chunk + 1) * chunk_cols]
            attn_part = add_out(attn_part, mine, own_rows)
            half = query_cols // 2
            other_rows = jnp.concatenate(
                [
                    jnp.where(core == 0, out_parts[1], out_parts[2]),
                    jnp.where(core == 0, out_parts[2], out_parts[1]),
                ]
            )[chunk * chunk_cols : (chunk + 1) * chunk_cols]
            attn_part = add_out(attn_part, got, other_rows)
        else:
            spread = lax.all_to_all(attended, "tensor", split_axis=2, concat_axis=1, tiled=True)
            rows = out_parts[0].reshape(tensor_size, chunks, chunk_cols, MODEL_WIDTH)[:, chunk]
            attn_part = add_out(
                attn_part, spread, rows.reshape(tensor_size * chunk_cols, MODEL_WIDTH)
            )

    own_tokens = tokens.transpose(1, 0, 2).reshape(local_reqs * local_rows, MODEL_WIDTH)
    residual = (own_tokens.astype(jnp.float32) + attn_part).astype(jnp.bfloat16)
    normed_mlp = norm_rows(residual, mlp_gain)
    mlp_part = jnp.zeros((local_reqs * local_rows, MODEL_WIDTH), jnp.float32)
    for gate, up, down in zip(gate_parts, up_parts, down_parts, strict=True):
        gate_part = jnp.dot(normed_mlp, gate, preferred_element_type=jnp.float32)
        up_part = jnp.dot(normed_mlp, up, preferred_element_type=jnp.float32)
        hidden = (jax.nn.silu(gate_part) * up_part).astype(jnp.bfloat16)
        mlp_part = mlp_part + jnp.dot(hidden, down, preferred_element_type=jnp.float32)
    result = (residual.astype(jnp.float32) + mlp_part).astype(jnp.bfloat16)
    return result.reshape(local_reqs, local_rows, MODEL_WIDTH).transpose(1, 0, 2)


def solution(mesh):
    in_specs = (
        P("tensor", "dp", None),
        P("dp"),
        P("dp"),
        P(),
        P(None, "tensor"),
        P(None, "tensor"),
        P(None, "tensor"),
        P("tensor", None),
        P("dp", None, "tensor"),
        P("dp", None, "tensor"),
        P(None, "dp", "tensor"),
        P(None, "dp", "tensor"),
        P(),
        P(None, "tensor"),
        P(None, "tensor"),
        P("tensor", None),
    )
    out_specs = P("tensor", "dp", None)
    return jax.shard_map(
        functools.partial(body, mesh.shape["dp"], mesh.shape["tensor"]),
        mesh=mesh,
        in_specs=in_specs,
        out_specs=out_specs,
        check_vma=False,
    )
```

time: 995 us -> 746 us (0.75)
  matrix products: 439 us -> 73.9 us
  waiting for transfers between devices: 153 us -> 376 us
  Pallas kernels: 0 us -> 198 us
  other arithmetic: 199 us -> 13.7 us
  local copies, waits for them, and re-layouts: 163 us -> 49.4 us
  loops' own time: 21.7 us -> 0 us
  starting transfers between devices: 0.2 us -> 10.7 us
    dot_general x41 -> x20, matrix products: 439 us -> 73.9 us  [the longest x3 34.6 us: body(): jnp.dot(hidden, down, preferred_element_type=jnp.float32)]
    ppermute x0 -> x11, waiting for transfers between devices: none -> 245 us  [the longest x4 211 us: fetch(): mine = lax.ppermute(sent, 'tensor', swap)]
    pallas_call x0 -> x2, Pallas kernels: none -> 198 us  [attend(): pl.pallas_call(attention_kernel, grid_spec=pltpu.PrefetchScalarGridSpec(n...]
    reduce_sum x17 -> x0, other arithmetic: 159 us -> none  [absorb(): jnp.sum(weights, axis=-1)]
    reduce_scatter x2 -> x0, waiting for transfers between devices: 87 us -> none  [body(): lax.psum_scatter(jnp.dot(picked.reshape(lax.axis_size('tensor') * local_r...]
    all_gather x4 -> x2, waiting for transfers between devices: 64.7 us -> 131 us  [body(): prompts.append(lax.all_gather(part, 'dp', axis=0))]
    gather x6 -> x0, local copies, waits for them, and re-layouts: 63.3 us -> none  [the longest x3 31.7 us: shared_block(): jnp.take(key_piece, selector, axis=0)]
    another operation x2 -> x0, loops' own time: 21.7 us -> none  [the longest x1 16 us: body(): lax.scan(window_step, soft_state, jnp.arange(WINDOW_SPAN // FRESH_TOKENS,...]
  transfers between devices with their start and end apart: 6 -> 13, of which waited for: 4 -> 10; matrix products, arithmetic and copies ran while one was open for 40% -> 12% of each run, Pallas kernels for 0% -> 27%
where the time goes in v1:
time: 746 us; the launch traced here: 736 us
  waiting for transfers between devices  376 us (50%)
  Pallas kernels  198 us (27%)
  matrix products  73.9 us (10%)
  local copies, waits for them, and re-layouts  49.4 us (7%)
  between operations  14.1 us (2%)
  other arithmetic  13.7 us (2%)
  starting transfers between devices  10.7 us (1%)
    ppermute x4, waiting for transfers between devices, fetch(): mine = lax.ppermute(sent, 'tensor', swap)  211 us
    pallas_call x2, Pallas kernels, attend(): pl.pallas_call(attention_kernel, grid_spec=pltpu.PrefetchScalarGridSpec(n...  198 us
    all_gather x2, waiting for transfers between devices, body(): prompts.append(lax.all_gather(part, 'dp', axis=0))  131 us
    dot_general x3, matrix products, body(): jnp.dot(hidden, down, preferred_element_type=jnp.float32)  34.6 us
    unnamed x67, local copies, waits for them, and re-layouts  30.4 us
    ppermute x1, waiting for transfers between devices, body(): other = lax.ppermute(source, 'tensor', swap)  17.4 us
    dot_general x3, matrix products, body(): up_part = jnp.dot(normed_mlp, up, preferred_element_type=jnp.float32)  15.7 us
  transfers between devices with their start and end apart: 13, of which 10 were waited for; matrix products, arithmetic and copies ran while one was open for 12% of the time, Pallas kernels for 27%

profile of v1, /device:TPU:0, one launch (start us, length us, event | category | flops | bytes accessed | tf_op | source)
XLA Modules:
  0.0 735.5 jit_solution(278242071154575603)
XLA Ops:
  6.5 2.7 copy.53
  9.3 2.6 copy.54
  11.8 3.8 pad_maximum_fusion.1
  15.7 131.4 %all-gather.4.cloned.1.call-done.prompt_ref = bf16[16,8,384,256]{3,2,1,0:T(8,128)(2,1)} async-done(((bf16[1,8,384,256]{3,2,1,0:T(8,128)(2,1)}), bf16[16,8,384,256]{3,2,1,0:T(8,128)(2,1)}) %all-gather.4.cloned.1.call-update) | async-done | bytes 25165840 | tf_op jit(solution)/shard_map/all_gather | solution.py:250
  148.5 1.5 collective-permute-start.2
  150.0 26.7 %collective-permute-done.2 = bf16[384,1536]{1,0:T(8,128)(2,1)S(1)} collective-permute-done((bf16[384,1536]{1,0:T(8,128)(2,1)S(1)}, bf16[384,1536]{1,0:T(8,128)(2,1)S(1)}, u32[]{:S(2)}, u32[]{:S(2)}) %collective-permute-start.2) | collective-permute-done | bytes 1179680 | tf_op jit(solution)/shard_map/ppermute | solution.py:268
  176.7 3.0 collective-permute-done.3
  179.6 2.3 constant_dynamic-slice_fusion.2
  181.9 1.5 collective-permute-start.5
  183.5 68.7 %collective-permute-done.5 = bf16[1536,1024]{1,0:T(8,128)(2,1)S(1)} collective-permute-done((bf16[1536,1024]{1,0:T(8,128)(2,1)S(1)}, bf16[1536,1024]{1,0:T(8,128)(2,1)S(1)}, u32[]{:S(2)}, u32[]{:S(2)}) %collective-permute-start.5) | collective-permute-done | bytes 3145760 | tf_op jit(solution)/shard_map/ppermute | solution.py:268
  252.1 1.7 copy-done.23
  253.8 4.1 collective-permute-done.6
  257.9 2.2 constant_dynamic-slice_fusion.1
  260.1 1.5 collective-permute-start.7
  261.7 68.9 %collective-permute-done.7 = bf16[1536,1024]{1,0:T(8,128)(2,1)} collective-permute-done((bf16[1536,1024]{1,0:T(8,128)(2,1)S(1)}, bf16[1536,1024]{1,0:T(8,128)(2,1)}, u32[]{:S(2)}, u32[]{:S(2)}) %collective-permute-start.7) | collective-permute-done | bytes 3145760 | tf_op jit(solution)/shard_map/ppermute | solution.py:268
  331.0 1.6 fusion.10
  334.1 8.7 %copy.51 = bf16[2,4096,384]{1,2,0:T(8,128)(2,1)} copy(bf16[2,4096,384]{2,1,0:T(8,128)(2,1)} %param.24) | data formatting | bytes 12582912 | tf_op args[8]
  342.8 8.7 %copy.52 = bf16[2,4096,384]{1,2,0:T(8,128)(2,1)} copy(bf16[2,4096,384]{2,1,0:T(8,128)(2,1)} %param.25) | data formatting | bytes 12582912 | tf_op args[9]
  352.4 17.4 %collective-permute-done = bf16[2,256,1536]{2,1,0:T(8,128)(2,1)} collective-permute-done((bf16[2,256,1536]{2,1,0:T(8,128)(2,1)}, bf16[2,256,1536]{2,1,0:T(8,128)(2,1)}, u32[]{:S(2)}, u32[]{:S(2)}) %collective-permute-start) | collective-permute-done | bytes 1572896 | tf_op jit(solution)/shard_map/ppermute | solution.py:254
  369.7 2.7 broadcast_select_fusion
  372.4 3.9 constant_dynamic-slice_fusion
  380.2 2.6 convolution_bitcast_fusion.1
  382.7 3.1 copy.44
  385.8 4.0 convolution_bitcast_fusion
  389.8 2.0 copy.45
  391.8 2.2 fusion.72
  399.1 47.2 %collective-permute-done.9 = bf16[1024,1536]{1,0:T(8,128)(2,1)} collective-permute-done((bf16[1024,1536]{1,0:T(8,128)(2,1)}, bf16[1024,1536]{1,0:T(8,128)(2,1)}, u32[]{:S(2)}, u32[]{:S(2)}) %collective-permute-start.9) | collective-permute-done | bytes 3145760 | tf_op jit(solution)/shard_map/ppermute | solution.py:268
  446.4 98.7 %attend.2 = bf16[2,384,512]{2,1,0:T(8,128)(2,1)S(1)} custom-call(s32[2]{0:T(128)S(1)} %copy-done.3, s32[2]{0:T(128)S(1)} %copy-done.4, bf16[2,768,512]{2,1,0:T(8,128)(2,1)S(1)} %bitcast.145, bf16[2,384,512]{2,1,0:T(8,128)(2,1)S(1)} %bitcast.147, bf16[2,384,512]{2,1,0:T(8,128)(2,1)S(1)} %pad_maximum_fusion.6.fresh_v_ref, bf16[2,384,4096]{2,1,0:T(8,128)(2,1)S(1)} %bitcast.143, ...), custom_call_target="tpu_custom_call" | custom-call | flops 19327352832 | bytes 25165824 | tf_op jit(solution)/shard_map/attend/pallas_call | solution.py:174
  545.1 1.5 collective-permute-start.1
  546.6 1.7 fusion.31
  548.3 1.8 fusion.29
  550.2 3.7 collective-permute-done.1
  553.9 1.8 fusion.37
  555.7 1.8 fusion.36
  557.5 2.8 copy-done.2
  560.2 99.0 %attend.3 = bf16[2,384,512]{2,1,0:T(8,128)(2,1)S(1)} custom-call(s32[2]{0:T(128)S(1)} %copy-done.3, s32[2]{0:T(128)S(1)} %copy-done.4, bf16[2,768,512]{2,1,0:T(8,128)(2,1)S(1)} %bitcast.146, bf16[2,384,512]{2,1,0:T(8,128)(2,1)S(1)} %bitcast.148, bf16[2,384,512]{2,1,0:T(8,128)(2,1)S(1)} %pad_maximum_fusion.6.fresh_v_ref, bf16[2,384,4096]{2,1,0:T(8,128)(2,1)S(1)} %bitcast.144, ...), custom_call_target="tpu_custom_call" | custom-call | flops 19327352832 | bytes 25165824 | tf_op jit(solution)/shard_map/attend/pallas_call | solution.py:174
  659.3 1.5 collective-permute-start.4
  662.0 5.1 collective-permute-done.4
  667.2 2.0 fusion.39
  669.2 2.0 fusion.38
  671.6 1.7 fusion.6
  674.0 5.2 fusion.51
  679.3 5.2 fusion.47
  684.5 5.3 fusion.55
  689.8 8.9 %fusion.21 = f32[512,1536]{1,0:T(8,128)} fusion(bf16[1024,1536]{1,0:T(8,128)(2,1)} %collective-permute-done.9, f32[512,1024]{1,0:T(8,128)} %fusion.51, bf16[1536,1024]{1,0:T(8,128)(2,1)} %copy-done.23, bf16[512,1536]{1,0:T(8,128)(2,1)S(1)} %get-tuple-element.17, f32[1536]{0:T(1024)S(1)} %copy-done.26, f32[512]{0:T(512)S(1)} %bitcast.166), kind=kOutput, calls=%fused_computation.58 | convolution fusion | flops 3227516928 | bytes 13115392 | tf_op jit(solution)/shard_map/dot_general | solution.py:356
  698.6 8.8 %fusion.22 = f32[512,1536]{1,0:T(8,128)} fusion(bf16[1024,1536]{1,0:T(8,128)(2,1)} %collective-permute-done.10, f32[512,1024]{1,0:T(8,128)} %fusion.47, bf16[1536,1024]{1,0:T(8,128)(2,1)} %collective-permute-done.6, bf16[512,1536]{1,0:T(8,128)(2,1)S(1)} %get-tuple-element.17, f32[1536]{0:T(1024)S(1)} %copy-done.26, f32[512]{0:T(512)S(1)} %bitcast.167), kind=kOutput, calls=%fused_computation.59 | convolution fusion | flops 3227516928 | bytes 13115392 | tf_op jit(solution)/shard_map/dot_general | solution.py:356
  707.4 16.9 %fusion.3 = bf16[512,1536]{1,0:T(8,128)(2,1)} fusion(bf16[512,1536]{1,0:T(8,128)(2,1)} %copy-done.17, f32[512,1536]{1,0:T(8,128)} %fusion.22, f32[512,1536]{1,0:T(8,128)} %fusion.21, bf16[2048,1536]{1,0:T(8,128)(2,1)} %param.31, f32[512,2048]{1,0:T(8,128)} %fusion.55, bf16[1536,2048]{1,0:T(8,128)(2,1)} %param.29, f32[1536]{0:T(1024)S(1)} %copy-done.26, ...), kind=kOutput, calls=%fused_computation.12 | convolution fusion | flops 6455820288 | bytes 26222592 | tf_op jit(solution)/shard_map/dot_general | solution.py:356
  724.3 4.2 copy.70
  (98 shorter events, 15.4 us)
Async XLA Ops:
  6.5 373.6 %copy-start = (bf16[1536,768]{1,0:T(8,128)(2,1)S(1)}, bf16[1536,768]{1,0:T(8,128)(2,1)}, u32[]{:S(2)}) copy-start(bf16[1536,768]{1,0:T(8,128)(2,1)} %param.20) | copy-start | bytes 7077892
  6.5 140.5 %all-gather.4.cloned.1.call-start = ((), (), s32[]{:S(2)}) async-start(), calls=%async_computation | async-start | bytes 26738688 | tf_op jit(solution)/shard_map/all_gather | solution.py:250
  15.6 541.8 %all-gather.6.cloned.1.call-start = ((), (), s32[]{:S(2)}) async-start(), calls=%async_computation.1 | async-start | bytes 26738688 | tf_op jit(solution)/shard_map/all_gather | solution.py:250
  148.5 28.2 %collective-permute-start.2 = (bf16[384,1536]{1,0:T(8,128)(2,1)S(1)}, bf16[384,1536]{1,0:T(8,128)(2,1)S(1)}, u32[]{:S(2)}, u32[]{:S(2)}) collective-permute-start(bf16[384,1536]{1,0:T(8,128)(2,1)S(1)} %constant_dynamic-slice_fusion.4), channel_id=1, source_target_pairs={{0,1},{1,0},{2,3},{3,2},{4,5},{5,4},{6,7},{7,6},{8,9},{9,8},{10,11... | collective-permute-start | bytes 3538952 | tf_op jit(solution)/shard_map/ppermute | solution.py:268
  176.7 5.2 copy-start.7
  176.7 3.0 collective-permute-start.3
  181.9 148.7 %copy-start.5 = (bf16[256,2,1536]{2,1,0:T(2,128)(2,1)S(1)}, bf16[256,2,1536]{2,1,0:T(2,128)(2,1)}, u32[]{:S(2)}) copy-start(bf16[256,2,1536]{2,1,0:T(2,128)(2,1)} %param.16) | copy-start | bytes 4718596
  181.9 149.1 %copy-start.22 = (f32[1536]{0:T(1024)S(1)}, f32[1536]{0:T(1024)}, u32[]{:S(2)}) copy-start(f32[1536]{0:T(1024)} %param.19) | copy-start | bytes 18436
  181.9 70.2 %collective-permute-start.5 = (bf16[1536,1024]{1,0:T(8,128)(2,1)S(1)}, bf16[1536,1024]{1,0:T(8,128)(2,1)S(1)}, u32[]{:S(2)}, u32[]{:S(2)}) collective-permute-start(bf16[1536,1024]{1,0:T(8,128)(2,1)S(1)} %constant_dynamic-slice_fusion.2), channel_id=1, source_target_pairs={{0,1},{1,0},{2,3},{3,2},{4,5},{5,4},{6,7},{7,6},{8,9},{9,8},{10,11... | collective-permute-start | bytes 9437192 | tf_op jit(solution)/shard_map/ppermute | solution.py:268
  252.1 1.7 copy-start.23
  252.1 5.8 collective-permute-start.6
  260.1 70.5 %collective-permute-start.7 = (bf16[1536,1024]{1,0:T(8,128)(2,1)S(1)}, bf16[1536,1024]{1,0:T(8,128)(2,1)}, u32[]{:S(2)}, u32[]{:S(2)}) collective-permute-start(bf16[1536,1024]{1,0:T(8,128)(2,1)S(1)} %constant_dynamic-slice_fusion.1), channel_id=1, source_target_pairs={{0,1},{1,0},{2,3},{3,2},{4,5},{5,4},{6,7},{7,6},{8,9},{9,8},{10,11... | collective-permute-start | bytes 9437192 | tf_op jit(solution)/shard_map/ppermute | solution.py:268
  330.6 41.8 %collective-permute-start.8 = (bf16[1536,1024]{1,0:T(8,128)(2,1)}, bf16[1536,1024]{1,0:T(8,128)(2,1)}, u32[]{:S(2)}, u32[]{:S(2)}) collective-permute-start(bf16[1536,1024]{1,0:T(8,128)(2,1)} %collective-permute-done.7), channel_id=1, source_target_pairs={{0,2},{2,0},{4,6},{6,4},{8,10},{10,8},{12,14},{14,12},{16,18},{18,... | collective-permute-start | bytes 9437192 | tf_op jit(solution)/shard_map/ppermute | solution.py:269
  332.6 37.1 %collective-permute-start = (bf16[2,256,1536]{2,1,0:T(8,128)(2,1)}, bf16[2,256,1536]{2,1,0:T(8,128)(2,1)}, u32[]{:S(2)}, u32[]{:S(2)}) collective-permute-start(bf16[2,256,1536]{2,1,0:T(8,128)(2,1)} %fusion.10), channel_id=1, source_target_pairs={{0,1},{1,0},{2,3},{3,2},{4,5},{5,4},{6,7},{7,6},{8,9},{9,8},{10,11... | collective-permute-start | bytes 4718600 | tf_op jit(solution)/shard_map/ppermute | solution.py:254
  342.8 8.7 %copy-start.4 = (s32[2]{0:T(128)S(1)}, s32[2]{0:T(128)}, u32[]{:S(2)}) copy-start(s32[2]{0:T(128)} %len_ref.3) | copy-start | bytes 28
  376.3 70.0 %collective-permute-start.9 = (bf16[1024,1536]{1,0:T(8,128)(2,1)}, bf16[1024,1536]{1,0:T(8,128)(2,1)}, u32[]{:S(2)}, u32[]{:S(2)}) collective-permute-start(bf16[1024,1536]{1,0:T(8,128)(2,1)} %constant_dynamic-slice_fusion), channel_id=1, source_target_pairs={{0,1},{1,0},{2,3},{3,2},{4,5},{5,4},{6,7},{7,6},{8,9},{9,8},{10,11... | collective-permute-start | bytes 9437192 | tf_op jit(solution)/shard_map/ppermute | solution.py:268
  379.0 1.2 copy-start.19
  389.8 2.0 copy-start.20
  391.8 2.3 copy-start.18
  391.8 2.3 copy-start.24
  394.9 1.4 copy-start.21
  394.9 1.7 copy-start.25
  396.6 1.8 copy-start.16
  397.5 48.9 %slice-start = ((s8[6291456]{0:T(1024)(128)(4,1)}), s8[4194304]{0:T(1024)(128)(4,1)S(1)}, s32[]{:S(2)}) async-start(s8[6291456]{0:T(1024)(128)(4,1)} %bitcast.141), calls=%async_computation.2 | async-start | bytes 8388608
  398.4 47.9 %slice-start.1 = ((s8[6291456]{0:T(1024)(128)(4,1)}), s8[2097152]{0:T(1024)(128)(4,1)S(1)}, s32[]{:S(2)}) async-start(s8[6291456]{0:T(1024)(128)(4,1)} %bitcast.141), calls=%async_computation.3 | async-start | bytes 4194304
  398.9 47.4 %copy-start.3 = (s32[2]{0:T(128)S(1)}, s32[2]{0:T(128)}, u32[]{:S(2)}) copy-start(s32[2]{0:T(128)} %group_ref.3) | copy-start | bytes 28
  446.3 252.3 %collective-permute-start.10 = (bf16[1024,1536]{1,0:T(8,128)(2,1)}, bf16[1024,1536]{1,0:T(8,128)(2,1)}, u32[]{:S(2)}, u32[]{:S(2)}) collective-permute-start(bf16[1024,1536]{1,0:T(8,128)(2,1)} %collective-permute-done.9), channel_id=1, source_target_pairs={{0,2},{2,0},{4,6},{6,4},{8,10},{10,8},{12,14},{14,12},{16,18},{18,... | collective-permute-start | bytes 9437192 | tf_op jit(solution)/shard_map/ppermute | solution.py:269
  446.3 100.3 %copy-start.10 = (bf16[768,1536]{1,0:T(8,128)(2,1)S(1)}, bf16[768,1536]{1,0:T(8,128)(2,1)}, u32[]{:S(2)}) copy-start(bf16[768,1536]{1,0:T(8,128)(2,1)} %param.23) | copy-start | bytes 7077892
  545.1 8.9 %collective-permute-start.1 = (bf16[2,384,256]{2,1,0:T(8,128)(2,1)S(1)}, bf16[2,384,256]{2,1,0:T(8,128)(2,1)S(1)}, u32[]{:S(2)}, u32[]{:S(2)}) collective-permute-start(bf16[2,384,256]{2,1,0:T(8,128)(2,1)S(1)} %constant_dynamic-slice_fusion.5), channel_id=1, source_target_pairs={{0,1},{1,0},{2,3},{3,2},{4,5},{5,4},{6,7},{7,6},{8,9},{9,8},{10,11... | collective-permute-start | bytes 1179656 | tf_op jit(solution)/shard_map/ppermute | solution.py:330
  548.3 5.6 copy-start.8
  557.5 2.8 copy-start.2
  560.2 100.6 %copy-start.11 = (bf16[768,1536]{1,0:T(8,128)(2,1)S(1)}, bf16[768,1536]{1,0:T(8,128)(2,1)}, u32[]{:S(2)}) copy-start(bf16[768,1536]{1,0:T(8,128)(2,1)} %param.23) | copy-start | bytes 7077892
  659.3 7.8 %collective-permute-start.4 = (bf16[2,384,256]{2,1,0:T(8,128)(2,1)S(1)}, bf16[2,384,256]{2,1,0:T(8,128)(2,1)S(1)}, u32[]{:S(2)}, u32[]{:S(2)}) collective-permute-start(bf16[2,384,256]{2,1,0:T(8,128)(2,1)S(1)} %constant_dynamic-slice_fusion.3), channel_id=1, source_target_pairs={{0,1},{1,0},{2,3},{3,2},{4,5},{5,4},{6,7},{7,6},{8,9},{9,8},{10,11... | collective-permute-start | bytes 1179656 | tf_op jit(solution)/shard_map/ppermute | solution.py:330
  661.4 5.7 copy-start.9
  667.1 4.1 copy-start.13
  667.1 4.1 copy-start.14
  667.1 4.2 copy-start.15
  669.2 2.1 copy-start.6
  669.2 2.4 copy-start.12
  673.3 25.3 %copy-start.17 = (bf16[512,1536]{1,0:T(8,128)(2,1)}, bf16[512,1536]{1,0:T(8,128)(2,1)S(1)}, u32[]{:S(2)}) copy-start(bf16[512,1536]{1,0:T(8,128)(2,1)S(1)} %get-tuple-element.17) | copy-start | bytes 4718596
  673.3 0.7 copy-start.26
  674.0 10.4 %slice-start.2 = ((s8[6291456]{0:T(1024)(128)(4,1)}), s8[4194304]{0:T(1024)(128)(4,1)S(1)}, s32[]{:S(2)}) async-start(s8[6291456]{0:T(1024)(128)(4,1)} %bitcast.158), calls=%async_computation.4 | async-start | bytes 8388608
  679.3 5.2 slice-start.3
  707.4 21.1 %copy-start.1 = (bf16[1536,768]{1,0:T(8,128)(2,1)S(1)}, bf16[1536,768]{1,0:T(8,128)(2,1)}, u32[]{:S(2)}) copy-start(bf16[1536,768]{1,0:T(8,128)(2,1)} %param.20) | copy-start | bytes 7077892
Sparse Core Ops, SparseCore 0:
  15.7 131.2 all-gather.3
  148.7 128.5 all-gather.5

commit v2 on v1

v2 whole, which is shorter than its diff:
```python
import functools
import math

import jax
import jax.numpy as jnp
from jax import lax
from jax.experimental import pallas as pl
from jax.experimental.pallas import tpu as pltpu
from jax.sharding import PartitionSpec as P

MODEL_WIDTH = 1536
HEAD_SIZE = 96
FRESH_TOKENS = 512
WINDOW_SPAN = 4096
SINKS = 4
PROMPT_TOKENS = 4096

rope_base = 10000.0
epsilon = 1e-05
far_below = -1e30
EXP2_SCALE = math.log2(math.e) / math.sqrt(HEAD_SIZE)
QUERY_TILE = 256
CACHE_BLOCK = 256
SUM_ROWS = 16


def norm_rows(values, gain_vec):
    widened = values.astype(jnp.float32)
    factor = lax.rsqrt(jnp.mean(widened * widened, axis=-1, keepdims=True) + epsilon)
    return (widened * factor * gain_vec).astype(jnp.bfloat16)


def rotate_columns(values, positions):
    requests, rows, tokens = values.shape
    half_dim = HEAD_SIZE // 2
    frequency = rope_base ** (-2.0 * jnp.arange(half_dim, dtype=jnp.float32) / HEAD_SIZE)
    angles = positions.astype(jnp.float32)[:, None, None, :] * frequency[None, None, :, None]
    cosine = jnp.cos(angles)
    sine_part = jnp.sin(angles)
    split = values.reshape(requests, rows // HEAD_SIZE, 2, half_dim, tokens)
    first_half = split[:, :, 0]
    second_half = split[:, :, 1]
    turned = jnp.concatenate(
        [
            first_half * cosine - second_half * sine_part,
            second_half * cosine + first_half * sine_part,
        ],
        axis=2,
    )
    return turned.astype(jnp.bfloat16).reshape(requests, rows, tokens)


def attention_kernel(
    group_ref,
    len_ref,
    q_ref,
    fresh_k_ref,
    fresh_v_ref,
    cache_k_ref,
    cache_v_ref,
    prompt_ref,
    out_ref,
    wide_ref,
    sum_ref,
    even_ref,
    odd_ref,
):
    length = len_ref[pl.program_id(0)]
    heads = q_ref.shape[1] // HEAD_SIZE
    pieces, piece = prompt_ref.shape[0], prompt_ref.shape[3]
    width = heads * FRESH_TOKENS
    tiles = [slice(start, start + QUERY_TILE) for start in range(0, width, QUERY_TILE)]
    for head in range(heads):
        wide_ref[:, head * FRESH_TOKENS : (head + 1) * FRESH_TOKENS] = q_ref[
            0, head * HEAD_SIZE : (head + 1) * HEAD_SIZE, :
        ]
    sum_ref[...] = jnp.zeros(sum_ref.shape, jnp.float32)

    def load_fresh(index):
        columns = slice(index * QUERY_TILE, (index + 1) * QUERY_TILE)
        return fresh_k_ref[0, :, columns], fresh_v_ref[0, :, columns]

    def load_cache(index):
        columns = pl.ds(pl.multiple_of(index * CACHE_BLOCK, CACHE_BLOCK), CACHE_BLOCK)
        return cache_k_ref[0, :, columns], cache_v_ref[0, :, columns]

    def load_prompt(index):
        return (
            prompt_ref[index, 0, 0:HEAD_SIZE, :],
            prompt_ref[index, 0, HEAD_SIZE : 2 * HEAD_SIZE, :],
        )

    def widen(values):
        return jnp.concatenate(
            [values, jnp.ones((SUM_ROWS, values.shape[1]), jnp.bfloat16)], axis=0
        )

    def digest(widened, scores, old_peak, tile):
        new_peak = jnp.maximum(old_peak, jnp.max(scores, axis=0, keepdims=True))
        weights = jnp.exp2((scores - new_peak) * EXP2_SCALE).astype(jnp.bfloat16)
        factor = jnp.exp2((old_peak - new_peak) * EXP2_SCALE)
        sum_ref[:, tile] = sum_ref[:, tile] * factor + jnp.dot(
            widened, weights, preferred_element_type=jnp.float32
        )
        return new_peak

    def masked_step(peak, loaded, visible, least=0):
        keys, values = loaded
        turned = keys.T
        widened = widen(values)
        scores = []
        for tile in tiles:
            raw = jnp.dot(turned, wide_ref[:, tile], preferred_element_type=jnp.float32)
            key_ids = lax.broadcasted_iota(jnp.int32, raw.shape, 0)
            row_ids = lax.broadcasted_iota(jnp.int32, raw.shape, 1) + tile.start % FRESH_TOKENS
            scores.append(jnp.where(visible(key_ids, row_ids), raw, far_below))
        peaks = []
        for tile, score in zip(tiles, scores, strict=True):
            old = peak[:, tile]
            if tile.start % FRESH_TOKENS + QUERY_TILE <= least:
                peaks.append(old)
            else:
                peaks.append(digest(widened, score, old, tile))
        return jnp.concatenate(peaks, axis=1)

    def masked(low, high, load, visible, peak):
        return lax.fori_loop(
            low, high, lambda index, peak: masked_step(peak, load(index), visible(index)), peak
        )

    def score_into(loaded, held_ref):
        turned = loaded[0].T
        for tile in tiles:
            held_ref[0 : turned.shape[0], tile] = jnp.dot(
                turned, wide_ref[:, tile], preferred_element_type=jnp.float32
            )

    def digest_all(loaded, peak, held_ref):
        widened = widen(loaded[1])
        block = widened.shape[1]
        return jnp.concatenate(
            [digest(widened, held_ref[0:block, tile], peak[:, tile], tile) for tile in tiles],
            axis=1,
        )

    def unmasked(low, high, load, peak):
        last = high - 1
        count = jnp.maximum(high - low, 0)

        def pair(step, peak):
            at = low + 2 * step
            score_into(load(at + 1), odd_ref)
            peak = digest_all(load(at), peak, even_ref)
            score_into(load(jnp.minimum(at + 2, last)), even_ref)
            return digest_all(load(at + 1), peak, odd_ref)

        @pl.when(count > 0)
        def _():
            score_into(load(low), even_ref)

        peak = lax.fori_loop(0, count // 2, pair, peak)
        return lax.fori_loop(
            0, count % 2, lambda _, peak: digest_all(load(last), peak, even_ref), peak
        )

    peak = jnp.full((1, width), far_below, jnp.float32)
    for index in range(FRESH_TOKENS // QUERY_TILE):
        start = index * QUERY_TILE
        peak = masked_step(
            peak,
            load_fresh(index),
            lambda keys, rows, start=start: keys + start <= rows,
            least=start,
        )

    cache_blocks = WINDOW_SPAN // CACHE_BLOCK
    first = jnp.maximum((WINDOW_SPAN - length) // CACHE_BLOCK, 0)
    clear = jnp.minimum(jnp.maximum(first + 1, FRESH_TOKENS // CACHE_BLOCK), cache_blocks)

    def cache_visible(index):
        start = index * CACHE_BLOCK
        return lambda keys, rows: (keys + start >= WINDOW_SPAN - length) & (keys + start > rows)

    def prompt_visible(index):
        start = index * piece
        return lambda keys, rows: (keys + start < SINKS) | (keys + start > length + rows)

    peak = masked(first, clear, load_cache, cache_visible, peak)
    peak = unmasked(clear, cache_blocks, load_cache, peak)
    peak = masked_step(peak, load_prompt(0), prompt_visible(0))
    begin = jnp.minimum(jnp.maximum((length + 1) // piece, 1), pieces)
    open_from = jnp.clip((length + FRESH_TOKENS - 1) // piece + 1, begin, pieces)
    peak = masked(begin, open_from, load_prompt, prompt_visible, peak)
    peak = unmasked(open_from, pieces, load_prompt, peak)

    for head in range(heads):
        total = sum_ref[:, head * FRESH_TOKENS : (head + 1) * FRESH_TOKENS]
        out_ref[0, head * HEAD_SIZE : (head + 1) * HEAD_SIZE, :] = (
            total[:HEAD_SIZE] / total[HEAD_SIZE : HEAD_SIZE + 1]
        ).astype(jnp.bfloat16)


def attend(groups, lengths, queries, fresh_k, fresh_v, cache_k, cache_v, prompts, first_head):
    requests = queries.shape[0]
    group_width = queries.shape[1] // cache_k.shape[1]
    heads = prompts.shape[2] // (2 * HEAD_SIZE)
    pieces, piece = prompts.shape[0], prompts.shape[3]
    query_rows = group_width * HEAD_SIZE
    own = lambda r, h, *_: (r, first_head + h, 0)
    width = group_width * FRESH_TOKENS
    return pl.pallas_call(
        attention_kernel,
        grid_spec=pltpu.PrefetchScalarGridSpec(
            num_scalar_prefetch=2,
            grid=(requests, heads),
            in_specs=[
                pl.BlockSpec((1, query_rows, FRESH_TOKENS), own),
                pl.BlockSpec((1, HEAD_SIZE, FRESH_TOKENS), own),
                pl.BlockSpec((1, HEAD_SIZE, FRESH_TOKENS), own),
                pl.BlockSpec((1, HEAD_SIZE, WINDOW_SPAN), own),
                pl.BlockSpec((1, HEAD_SIZE, WINDOW_SPAN), own),
                pl.BlockSpec(
                    (pieces, 1, 2 * HEAD_SIZE, piece), lambda r, h, group, _: (0, group[r], h, 0)
                ),
            ],
            out_specs=pl.BlockSpec((1, query_rows, FRESH_TOKENS), lambda r, h, *_: (r, h, 0)),
            scratch_shapes=[
                pltpu.VMEM((HEAD_SIZE, width), jnp.bfloat16),
                pltpu.VMEM((HEAD_SIZE + SUM_ROWS, width), jnp.float32),
                pltpu.VMEM((CACHE_BLOCK, width), jnp.float32),
                pltpu.VMEM((CACHE_BLOCK, width), jnp.float32),
            ],
        ),
        out_shape=jax.ShapeDtypeStruct((requests, heads * query_rows, FRESH_TOKENS), jnp.bfloat16),
        compiler_params=pltpu.CompilerParams(
            dimension_semantics=("arbitrary", "arbitrary"), vmem_limit_bytes=40 * 1024 * 1024
        ),
        cost_estimate=pl.CostEstimate(flops=1, bytes_accessed=1, transcendentals=0),
        name="attend",
    )(groups, lengths, queries, fresh_k, fresh_v, cache_k, cache_v, prompts)


def body(
    dp_size,
    tensor_size,
    tokens,
    cached_len,
    prompt_group,
    attn_gain,
    w_query,
    key_matrix,
    value_matrix,
    w_out,
    window_cache_keys,
    window_cache_values,
    prompt_keys,
    prompt_values,
    mlp_gain,
    w_gate,
    w_up,
    w_down,
):
    local_rows, local_reqs = tokens.shape[:2]
    query_cols = w_query.shape[1]
    key_cols = key_matrix.shape[1]
    key_heads = key_cols // HEAD_SIZE
    paired = tensor_size == 2 and dp_size % 2 == 0
    swap = [(0, 1), (1, 0)]
    across = [(rank, rank ^ 1) for rank in range(dp_size)]
    tensor_rank = lax.axis_index("tensor")
    core = lax.axis_index("dp") % 2

    chunk_heads = max(key_heads // 2, 1)
    chunks = key_heads // chunk_heads
    group_count, piece = prompt_keys.shape[:2]
    by_head = lambda a: a.transpose(0, 2, 1).reshape(group_count, key_heads, HEAD_SIZE, piece)
    packed = jnp.concatenate([by_head(prompt_keys), by_head(prompt_values)], axis=2)
    parts = [
        packed[:, chunk * chunk_heads : (chunk + 1) * chunk_heads].reshape(
            group_count, chunk_heads * 2 * HEAD_SIZE, piece
        )
        for chunk in range(chunks)
    ]
    prompts = [lax.all_gather(parts[0], "dp", axis=0)]

    source = norm_rows(tokens.transpose(1, 0, 2), attn_gain)
    weights = [w_gate, w_out, w_up, w_down]
    weight_axes = [1, 0, 1, 0]
    if paired:
        other = lax.ppermute(source, "tensor", swap)
        sent = []
        for weight, axis in zip(weights, weight_axes, strict=True):
            half = weight.shape[axis] // 2
            sent.append(lax.dynamic_slice_in_dim(weight, core * half, half, axis))
        other, *sent = lax.optimization_barrier((other, *sent))
        fetched = [lax.ppermute(sent[0], "tensor", swap)]
        low = tensor_rank == 0
        normed = jnp.concatenate(
            [jnp.where(low, source, other), jnp.where(low, other, source)], axis=1
        )
    else:
        fetched = []
        normed = lax.all_gather(source, "tensor", axis=1, tiled=True)
        weights = [
            lax.all_gather(weight, "tensor", axis=axis, tiled=True)
            for weight, axis in zip(weights, weight_axes, strict=True)
        ]

    positions = (
        PROMPT_TOKENS + cached_len[:, None] + jnp.arange(FRESH_TOKENS, dtype=jnp.int32)[None, :]
    )

    def project(weight):
        return jnp.stack(
            [
                lax.dot_general(
                    weight,
                    normed[request],
                    (((0,), (1,)), ((), ())),
                    preferred_element_type=jnp.float32,
                )
                for request in range(local_reqs)
            ]
        )

    queries = rotate_columns(project(w_query), positions)
    fresh_keys = rotate_columns(project(key_matrix), positions)
    fresh_values = project(value_matrix).astype(jnp.bfloat16)
    past_keys = window_cache_keys.transpose(0, 2, 1)
    past_values = window_cache_values.transpose(0, 2, 1)

    held = (prompts[0], queries, fresh_keys, fresh_values, past_keys, past_values)
    if paired:
        parts[1:], held, fetched, sent[1:] = lax.optimization_barrier(
            (parts[1:], held, fetched, sent[1:])
        )
        fetched += [lax.ppermute(part, "tensor", swap) for part in sent[1:]]
    else:
        parts[1:], held = lax.optimization_barrier((parts[1:], held))
    prompts[0], queries, fresh_keys, fresh_values, past_keys, past_values = held
    prompts += [lax.all_gather(part, "dp", axis=0) for part in parts[1:]]

    chunk_cols = query_cols // chunks
    attn_part = jnp.zeros((local_reqs * local_rows, MODEL_WIDTH), jnp.float32)

    def add_out(total, attended, weight):
        return total + jnp.concatenate(
            [
                lax.dot_general(
                    attended[request],
                    weight,
                    (((0,), (0,)), ((), ())),
                    preferred_element_type=jnp.float32,
                )
                for request in range(local_reqs)
            ]
        )

    parts_of = lambda chunk: slice(chunk * chunk_cols, (chunk + 1) * chunk_cols)
    swapped = []
    for chunk in range(chunks):
        attended = attend(
            prompt_group,
            cached_len,
            queries,
            fresh_keys,
            fresh_values,
            past_keys,
            past_values,
            prompts[chunk],
            chunk * chunk_heads,
        )
        if paired:
            if chunk == chunks - 1:
                attended, swapped, fetched = lax.optimization_barrier((attended, swapped, fetched))
            sent = lax.dynamic_slice_in_dim(attended, (1 - tensor_rank) * local_rows, local_rows, 2)
            swapped.append(lax.ppermute(sent, "tensor", swap))
            mine = lax.dynamic_slice_in_dim(attended, tensor_rank * local_rows, local_rows, 2)
            attn_part = add_out(attn_part, mine, w_out[parts_of(chunk)])
        else:
            spread = lax.all_to_all(attended, "tensor", split_axis=2, concat_axis=1, tiled=True)
            rows = weights[1].reshape(tensor_size, chunks, chunk_cols, MODEL_WIDTH)[:, chunk]
            attn_part = add_out(
                attn_part, spread, rows.reshape(tensor_size * chunk_cols, MODEL_WIDTH)
            )
    hidden_sets = [(weights[0], *weights[2:])]
    if paired:
        passed = [lax.ppermute(part, "dp", across) for part in fetched]
        hidden_sets += [(fetched[0], *fetched[2:]), (passed[0], *passed[2:])]
        first_core = core == 0
        other_out = jnp.concatenate(
            [
                jnp.where(first_core, fetched[1], passed[1]),
                jnp.where(first_core, passed[1], fetched[1]),
            ]
        )
        for chunk in range(chunks):
            attn_part = add_out(attn_part, swapped[chunk], other_out[parts_of(chunk)])

    own_tokens = tokens.transpose(1, 0, 2).reshape(local_reqs * local_rows, MODEL_WIDTH)
    residual = (own_tokens.astype(jnp.float32) + attn_part).astype(jnp.bfloat16)
    normed_mlp = norm_rows(residual, mlp_gain)
    mlp_part = jnp.zeros((local_reqs * local_rows, MODEL_WIDTH), jnp.float32)
    for gate, up, down in hidden_sets:
        gate_part = jnp.dot(normed_mlp, gate, preferred_element_type=jnp.float32)
        up_part = jnp.dot(normed_mlp, up, preferred_element_type=jnp.float32)
        hidden = (jax.nn.silu(gate_part) * up_part).astype(jnp.bfloat16)
        mlp_part = mlp_part + jnp.dot(hidden, down, preferred_element_type=jnp.float32)
    result = (residual.astype(jnp.float32) + mlp_part).astype(jnp.bfloat16)
    return result.reshape(local_reqs, local_rows, MODEL_WIDTH).transpose(1, 0, 2)


def solution(mesh):
    in_specs = (
        P("tensor", "dp", None),
        P("dp"),
        P("dp"),
        P(),
        P(None, "tensor"),
        P(None, "tensor"),
        P(None, "tensor"),
        P("tensor", None),
        P("dp", None, "tensor"),
        P("dp", None, "tensor"),
        P(None, "dp", "tensor"),
        P(None, "dp", "tensor"),
        P(),
        P(None, "tensor"),
        P(None, "tensor"),
        P("tensor", None),
    )
    out_specs = P("tensor", "dp", None)
    return jax.shard_map(
        functools.partial(body, mesh.shape["dp"], mesh.shape["tensor"]),
        mesh=mesh,
        in_specs=in_specs,
        out_specs=out_specs,
        check_vma=False,
    )
```

time: 746 us -> 414 us (0.55)
  waiting for transfers between devices: 376 us -> 162 us
  Pallas kernels: 198 us -> 71 us
    ppermute x10, waiting for transfers between devices: 227 us -> 51.2 us  [the longest x1 39.7 us: body(): fetched = [lax.ppermute(sent[0], 'tensor', swap)]]
    pallas_call x2, Pallas kernels: 198 us -> 71 us  [attend(): pl.pallas_call(attention_kernel, grid_spec=pltpu.PrefetchScalarGridSpec(n...]
    all_gather x2, waiting for transfers between devices: 131 us -> 107 us  [the longest x1 86.3 us: body(): prompts += [lax.all_gather(part, 'dp', axis=0) for part in parts[1:]]]
    dot_general x0 -> x1, matrix products: none -> 14.8 us  [body(): gate_part = jnp.dot(normed_mlp, gate, preferred_element_type=jnp.float32)]
    ppermute x1, waiting for transfers between devices: 17.4 us -> 3.8 us  [body(): other = lax.ppermute(source, 'tensor', swap)]
    dot_general x3 -> x2, matrix products: 15.7 us -> 10.2 us  [body(): up_part = jnp.dot(normed_mlp, up, preferred_element_type=jnp.float32)]
    unnamed x67 -> x47, local copies, waits for them, and re-layouts: 30.4 us -> 32.8 us
  transfers between devices with their start and end apart: 13 -> 13, of which waited for: 10 -> 6; matrix products, arithmetic and copies ran while one was open for 12% -> 29% of each run, Pallas kernels for 27% -> 17%
where the time goes in v2:
time: 414 us; the launch traced here: 409 us
  waiting for transfers between devices  162 us (39%)
  matrix products  78.9 us (19%)
  Pallas kernels  71 us (17%)
  local copies, waits for them, and re-layouts  55.6 us (13%)
  other arithmetic  17 us (4%)
  between operations  14 us (3%)
  starting transfers between devices  10.7 us (3%)
    all_gather x1, waiting for transfers between devices, body(): prompts += [lax.all_gather(part, 'dp', axis=0) for part in parts[1:]]  86.3 us
    pallas_call x2, Pallas kernels, attend(): pl.pallas_call(attention_kernel, grid_spec=pltpu.PrefetchScalarGridSpec(n...  71 us
    ppermute x1, waiting for transfers between devices, body(): fetched = [lax.ppermute(sent[0], 'tensor', swap)]  39.7 us
    dot_general x3, matrix products, body(): jnp.dot(hidden, down, preferred_element_type=jnp.float32)  33.3 us
    unnamed x47, local copies, waits for them, and re-layouts  32.8 us
    all_gather x1, waiting for transfers between devices, body(): prompts = [lax.all_gather(parts[0], 'dp', axis=0)]  20.6 us
    dot_general x1, matrix products, body(): gate_part = jnp.dot(normed_mlp, gate, preferred_element_type=jnp.float32)  14.8 us
    dot_general x6, matrix products, project(): lax.dot_general(weight, normed[request], (((0,), (1,)), ((), ())), prefer...  13.1 us
  transfers between devices with their start and end apart: 13, of which 6 were waited for; matrix products, arithmetic and copies ran while one was open for 29% of the time, Pallas kernels for 17%

profile of v2, /device:TPU:0, one launch (start us, length us, event | category | flops | bytes accessed | tf_op | source)
XLA Modules:
  0.0 409.2 jit_solution(5700442532016426241)
XLA Ops:
  6.5 2.7 copy.44
  9.3 2.6 copy.45
  11.9 3.9 pad_maximum_fusion.2
  15.8 1.9 fusion.7
  17.8 1.6 fusion.9
  19.3 3.0 collective-permute-start
  22.3 8.5 %copy.53 = bf16[2,4096,384]{1,2,0:T(8,128)(2,1)} copy(bf16[2,4096,384]{2,1,0:T(8,128)(2,1)} %param.24) | data formatting | bytes 12582912 | tf_op args[8]
  30.8 8.8 %copy.54 = bf16[2,4096,384]{1,2,0:T(8,128)(2,1)} copy(bf16[2,4096,384]{2,1,0:T(8,128)(2,1)} %param.25) | data formatting | bytes 12582912 | tf_op args[9]
  40.5 2.5 constant_dynamic-slice_fusion.4
  43.0 3.8 constant_dynamic-slice_fusion.2
  46.8 6.4 %constant_dynamic-slice_fusion.3 = (bf16[1536,1024]{1,0:T(8,128)(2,1)}, bf16[1536,1024]{1,0:T(8,128)(2,1)}) fusion(bf16[1536,2048]{1,0:T(8,128)(2,1)} %param.30, s32[]{:T(128)S(6)} %select_n.49, bf16[1536,2048]{1,0:T(8,128)(2,1)} %param.29), kind=kLoop, calls=%fused_computation.98 | loop fusion | bytes 12582916 | tf_op jit(solution)/shard_map/dynamic_slice | solution.py:294
  53.2 3.8 collective-permute-done
  57.0 1.7 collective-permute-start.1
  58.8 3.9 broadcast_select_fusion.1
  62.7 3.9 convolution_bitcast_fusion
  66.6 3.1 copy.47
  69.7 1.6 fusion.13
  71.3 1.1 copy-done.13
  72.4 2.6 convolution_bitcast_fusion.1
  75.1 1.9 copy.46
  77.0 2.7 fusion.18
  79.7 0.8 fusion.17
  80.7 1.2 copy-done.15
  81.8 2.2 fusion.49
  85.2 1.0 copy-done.12
  86.9 39.7 %collective-permute-done.1 = bf16[1536,1024]{1,0:T(8,128)(2,1)} collective-permute-done((bf16[1536,1024]{1,0:T(8,128)(2,1)}, bf16[1536,1024]{1,0:T(8,128)(2,1)}, u32[]{:S(2)}, u32[]{:S(2)}) %collective-permute-start.1) | collective-permute-done | bytes 3145760 | tf_op jit(solution)/shard_map/ppermute | solution.py:296
  126.6 20.6 %all-gather.4.cloned.1.call-done.prompt_ref = bf16[16,8,384,256]{3,2,1,0:T(8,128)(2,1)} async-done(((bf16[1,8,384,256]{3,2,1,0:T(8,128)(2,1)}), bf16[16,8,384,256]{3,2,1,0:T(8,128)(2,1)}) %all-gather.4.cloned.1.call-update) | async-done | bytes 25165840 | tf_op jit(solution)/shard_map/all_gather | solution.py:284
  147.2 1.5 collective-permute-start.4
  149.3 1.5 collective-permute-start.3
  150.8 2.8 copy-done.2
  153.6 35.8 %attend.2 = bf16[2,384,512]{2,1,0:T(8,128)(2,1)S(1)} custom-call(s32[2]{0:T(128)S(1)} %copy-done.6, s32[2]{0:T(128)S(1)} %copy-done.7, bf16[2,768,512]{2,1,0:T(8,128)(2,1)S(1)} %bitcast.143, bf16[2,384,512]{2,1,0:T(8,128)(2,1)S(1)} %bitcast.145, bf16[2,384,512]{2,1,0:T(8,128)(2,1)S(1)} %pad_maximum_fusion.6.fresh_v_ref, bf16[2,384,4096]{2,1,0:T(8,128)(2,1)S(1)} %bitcast.141, ...), custom_call_target="tpu_custom_call" | custom-call | flops 1 | bytes 1 | tf_op jit(solution)/shard_map/attend/pallas_call | solution.py:211
  189.4 0.9 copy-done.4
  191.1 86.3 %all-gather.6.cloned.1.call-done = bf16[128,384,256]{2,1,0:T(8,128)(2,1)} async-done(((bf16[8,384,256]{2,1,0:T(8,128)(2,1)}), bf16[128,384,256]{2,1,0:T(8,128)(2,1)}) %all-gather.6.cloned.1.call-update) | async-done | bytes 25165840 | tf_op jit(solution)/shard_map/all_gather | solution.py:341
  277.4 2.8 copy-done.3
  280.2 35.2 %attend.3 = bf16[2,384,512]{2,1,0:T(8,128)(2,1)S(1)} custom-call(s32[2]{0:T(128)S(1)} %copy-done.6, s32[2]{0:T(128)S(1)} %copy-done.7, bf16[2,768,512]{2,1,0:T(8,128)(2,1)S(1)} %bitcast.144, bf16[2,384,512]{2,1,0:T(8,128)(2,1)S(1)} %bitcast.146, bf16[2,384,512]{2,1,0:T(8,128)(2,1)S(1)} %pad_maximum_fusion.6.fresh_v_ref, bf16[2,384,4096]{2,1,0:T(8,128)(2,1)S(1)} %bitcast.142, ...), custom_call_target="tpu_custom_call" | custom-call | flops 1 | bytes 1 | tf_op jit(solution)/shard_map/attend/pallas_call | solution.py:211
  315.4 3.5 collective-permute-done.2
  320.3 1.6 collective-permute-start.7
  323.8 8.0 %collective-permute-done.7 = bf16[2,384,256]{2,1,0:T(8,128)(2,1)S(1)} collective-permute-done((bf16[2,384,256]{2,1,0:T(8,128)(2,1)S(1)}, bf16[2,384,256]{2,1,0:T(8,128)(2,1)S(1)}, u32[]{:S(2)}, u32[]{:S(2)}) %collective-permute-start.7) | collective-permute-done | bytes 393248 | tf_op jit(solution)/shard_map/ppermute | solution.py:377
  333.1 1.9 fusion.33
  335.0 2.0 fusion.34
  337.1 1.8 fusion.5
  339.6 14.8 %fusion.62 = f32[512,2048]{1,0:T(8,128)} fusion(bf16[1536,2048]{1,0:T(8,128)(2,1)S(1)} %bitcast.160, bf16[512,1536]{1,0:T(8,128)(2,1)S(1)} %get-tuple-element.49, f32[1536]{0:T(1024)S(1)} %copy-done.18, f32[512]{0:T(512)S(1)} %bitcast.162), kind=kOutput, calls=%fused_computation.113 | convolution fusion | flops 3224371200 | bytes 12066816 | tf_op jit(solution)/shard_map/dot_general | solution.py:405
  354.4 5.1 %fusion.56 = f32[512,1024]{1,0:T(8,128)} fusion(bf16[1536,1024]{1,0:T(8,128)(2,1)} %collective-permute-done.4, bf16[512,1536]{1,0:T(8,128)(2,1)S(1)} %get-tuple-element.49, f32[1536]{0:T(1024)S(1)} %copy-done.18, f32[512]{0:T(512)S(1)} %bitcast.163), kind=kOutput, calls=%fused_computation.111 | convolution fusion | flops 1613758464 | bytes 6823936 | tf_op jit(solution)/shard_map/dot_general | solution.py:406
  359.5 14.3 %fusion.19 = f32[512,1536]{1,0:T(8,128)} fusion(bf16[2048,1536]{1,0:T(8,128)(2,1)} %param.31, f32[512,2048]{1,0:T(8,128)} %fusion.62, bf16[1536,2048]{1,0:T(8,128)(2,1)} %param.30, bf16[512,1536]{1,0:T(8,128)(2,1)S(1)} %get-tuple-element.49, f32[1536]{0:T(1024)S(1)} %copy-done.18, f32[512]{0:T(512)S(1)} %bitcast.164), kind=kOutput, calls=%fused_computation.55 | convolution fusion | flops 6451888128 | bytes 21504000 | tf_op jit(solution)/shard_map/dot_general | solution.py:408
  373.8 9.8 %convolution_add_fusion.1 = f32[512,1536]{1,0:T(8,128)} fusion(f32[512,1536]{1,0:T(8,128)} %fusion.19, bf16[1024,1536]{1,0:T(8,128)(2,1)} %collective-permute-done.5, f32[512,1024]{1,0:T(8,128)} %fusion.56, bf16[1536,1024]{1,0:T(8,128)(2,1)} %collective-permute-done.1, bf16[512,1536]{1,0:T(8,128)(2,1)S(1)} %get-tuple-element.49, f32[1536]{0:T(1024)S(1)} %copy-done.18, ...), kind=kOutput, calls=%fused_computation.4 | convolution fusion | flops 3228303360 | bytes 16261120 | tf_op jit(solution)/shard_map/dot_general | solution.py:408
  383.6 5.1 %fusion.52 = f32[512,1024]{1,0:T(8,128)} fusion(bf16[1536,1024]{1,0:T(8,128)(2,1)} %collective-permute-done.9, bf16[512,1536]{1,0:T(8,128)(2,1)S(1)} %get-tuple-element.49, f32[1536]{0:T(1024)S(1)} %copy-done.18, f32[512]{0:T(512)S(1)} %bitcast.166), kind=kOutput, calls=%fused_computation.109 | convolution fusion | flops 1613758464 | bytes 6823936 | tf_op jit(solution)/shard_map/dot_general | solution.py:406
  388.7 9.2 %fusion.2 = bf16[512,1536]{1,0:T(8,128)(2,1)} fusion(bf16[512,1536]{1,0:T(8,128)(2,1)S(1)} %get-tuple-element.49, f32[512,1536]{1,0:T(8,128)} %convolution_add_fusion.1, bf16[1024,1536]{1,0:T(8,128)(2,1)} %collective-permute-done.10, f32[512,1024]{1,0:T(8,128)} %fusion.52, bf16[1536,1024]{1,0:T(8,128)(2,1)} %collective-permute-done.8, ...), kind=kOutput, calls=%fused_computation.7 | convolution fusion | flops 3230662656 | bytes 14688256 | tf_op jit(solution)/shard_map/dot_general | solution.py:408
  397.9 4.3 %copy.70 = bf16[2,256,1536]{2,0,1:T(2,128)(2,1)} copy(bf16[2,256,1536]{2,1,0:T(8,128)(2,1)} %bitcast.158) | data formatting | bytes 3145728 | tf_op jit(solution)/shard_map/reshape | solution.py:410
  (76 shorter events, 9.4 us)
Async XLA Ops:
  6.5 56.1 %copy-start = (bf16[1536,768]{1,0:T(8,128)(2,1)S(1)}, bf16[1536,768]{1,0:T(8,128)(2,1)}, u32[]{:S(2)}) copy-start(bf16[1536,768]{1,0:T(8,128)(2,1)} %param.20) | copy-start | bytes 7077892
  6.5 140.7 %all-gather.4.cloned.1.call-start = ((), (), s32[]{:S(2)}) async-start(), calls=%async_computation | async-start | bytes 26738688 | tf_op jit(solution)/shard_map/all_gather | solution.py:284
  15.7 2.0 copy-start.16
  15.8 261.7 %all-gather.6.cloned.1.call-start = ((), (), s32[]{:S(2)}) async-start(), calls=%async_computation.1 | async-start | bytes 26738688 | tf_op jit(solution)/shard_map/all_gather | solution.py:341
  15.8 1.9 copy-start.8
  19.3 37.7 %collective-permute-start = (bf16[2,256,1536]{2,1,0:T(8,128)(2,1)}, bf16[2,256,1536]{2,1,0:T(8,128)(2,1)}, u32[]{:S(2)}, u32[]{:S(2)}) collective-permute-start(bf16[2,256,1536]{2,1,0:T(8,128)(2,1)} %fusion.9), channel_id=1, source_target_pairs={{0,1},{1,0},{2,3},{3,2},{4,5},{5,4},{6,7},{7,6},{8,9},{9,8},{10,11... | collective-permute-start | bytes 4718600 | tf_op jit(solution)/shard_map/ppermute | solution.py:290
  30.8 8.9 %copy-start.7 = (s32[2]{0:T(128)S(1)}, s32[2]{0:T(128)}, u32[]{:S(2)}) copy-start(s32[2]{0:T(128)} %len_ref.3) | copy-start | bytes 28
  46.8 11.9 %copy-start.9 = (bf16[256,2,1536]{2,1,0:T(2,128)(2,1)S(1)}, bf16[256,2,1536]{2,1,0:T(2,128)(2,1)}, u32[]{:S(2)}) copy-start(bf16[256,2,1536]{2,1,0:T(2,128)(2,1)} %param.16) | copy-start | bytes 4718596
  57.0 69.6 %collective-permute-start.1 = (bf16[1536,1024]{1,0:T(8,128)(2,1)}, bf16[1536,1024]{1,0:T(8,128)(2,1)}, u32[]{:S(2)}, u32[]{:S(2)}) collective-permute-start(bf16[1536,1024]{1,0:T(8,128)(2,1)} %get-tuple-element.28), channel_id=1, source_target_pairs={{0,1},{1,0},{2,3},{3,2},{4,5},{5,4},{6,7},{7,6},{8,9},{9,8},{10,11... | collective-permute-start | bytes 9437192 | tf_op jit(solution)/shard_map/ppermute | solution.py:296
  71.3 1.1 copy-start.13
  77.0 2.7 copy-start.14
  77.0 2.7 copy-start.17
  80.6 1.3 copy-start.15
  84.8 1.4 copy-start.12
  86.9 63.9 %copy-start.6 = (s32[2]{0:T(128)S(1)}, s32[2]{0:T(128)}, u32[]{:S(2)}) copy-start(s32[2]{0:T(128)} %group_ref.3) | copy-start | bytes 28
  147.2 171.7 %collective-permute-start.4 = (bf16[1536,1024]{1,0:T(8,128)(2,1)}, bf16[1536,1024]{1,0:T(8,128)(2,1)}, u32[]{:S(2)}, u32[]{:S(2)}) collective-permute-start(bf16[1536,1024]{1,0:T(8,128)(2,1)} %get-tuple-element.41), channel_id=1, source_target_pairs={{0,1},{1,0},{2,3},{3,2},{4,5},{5,4},{6,7},{7,6},{8,9},{9,8},{10,11... | collective-permute-start | bytes 9437192 | tf_op jit(solution)/shard_map/ppermute | solution.py:337
  148.8 170.1 %collective-permute-start.5 = (bf16[1024,1536]{1,0:T(8,128)(2,1)}, bf16[1024,1536]{1,0:T(8,128)(2,1)}, u32[]{:S(2)}, u32[]{:S(2)}) collective-permute-start(bf16[1024,1536]{1,0:T(8,128)(2,1)} %constant_dynamic-slice_fusion.2), channel_id=1, source_target_pairs={{0,1},{1,0},{2,3},{3,2},{4,5},{5,4},{6,7},{7,6},{8,9},{9,8},{10,11... | collective-permute-start | bytes 9437192 | tf_op jit(solution)/shard_map/ppermute | solution.py:337
  149.3 169.6 %collective-permute-start.3 = (bf16[384,1536]{1,0:T(8,128)(2,1)}, bf16[384,1536]{1,0:T(8,128)(2,1)}, u32[]{:S(2)}, u32[]{:S(2)}) collective-permute-start(bf16[384,1536]{1,0:T(8,128)(2,1)} %constant_dynamic-slice_fusion.4), channel_id=1, source_target_pairs={{0,1},{1,0},{2,3},{3,2},{4,5},{5,4},{6,7},{7,6},{8,9},{9,8},{10,11... | collective-permute-start | bytes 3538952 | tf_op jit(solution)/shard_map/ppermute | solution.py:337
  150.8 2.8 copy-start.2
  189.4 0.9 copy-start.4
  191.1 127.8 %collective-permute-start.2 = (bf16[2,384,256]{2,1,0:T(8,128)(2,1)}, bf16[2,384,256]{2,1,0:T(8,128)(2,1)S(1)}, u32[]{:S(2)}, u32[]{:S(2)}) collective-permute-start(bf16[2,384,256]{2,1,0:T(8,128)(2,1)} %constant_dynamic-slice_fusion.1), channel_id=1, source_target_pairs={{0,1},{1,0},{2,3},{3,2},{4,5},{5,4},{6,7},{7,6},{8,9},{9,8},{10,11... | collective-permute-start | bytes 1179656 | tf_op jit(solution)/shard_map/ppermute | solution.py:377
  277.4 2.8 copy-start.3
  280.2 38.8 %copy-start.5 = (bf16[2,384,512]{2,1,0:T(8,128)(2,1)S(1)}, bf16[2,384,512]{2,1,0:T(8,128)(2,1)}, u32[]{:S(2)}) copy-start(bf16[2,384,512]{2,1,0:T(8,128)(2,1)} %copy-done.4) | copy-start | bytes 2359300
  280.2 38.8 %copy-start.11 = (bf16[768,1536]{1,0:T(8,128)(2,1)S(1)}, bf16[768,1536]{1,0:T(8,128)(2,1)}, u32[]{:S(2)}) copy-start(bf16[768,1536]{1,0:T(8,128)(2,1)} %param.23) | copy-start | bytes 7077892
  318.9 12.9 %collective-permute-start.6 = (bf16[384,1536]{1,0:T(8,128)(2,1)}, bf16[384,1536]{1,0:T(8,128)(2,1)S(1)}, u32[]{:S(2)}, u32[]{:S(2)}) collective-permute-start(bf16[384,1536]{1,0:T(8,128)(2,1)} %collective-permute-done.3), channel_id=1, source_target_pairs={{0,2},{2,0},{4,6},{6,4},{8,10},{10,8},{12,14},{14,12},{16,18},{18,... | collective-permute-start | bytes 3538952 | tf_op jit(solution)/shard_map/ppermute | solution.py:388
  320.3 11.6 %collective-permute-start.7 = (bf16[2,384,256]{2,1,0:T(8,128)(2,1)S(1)}, bf16[2,384,256]{2,1,0:T(8,128)(2,1)S(1)}, u32[]{:S(2)}, u32[]{:S(2)}) collective-permute-start(bf16[2,384,256]{2,1,0:T(8,128)(2,1)S(1)} %constant_dynamic-slice_fusion), channel_id=1, source_target_pairs={{0,1},{1,0},{2,3},{3,2},{4,5},{5,4},{6,7},{7,6},{8,9},{9,8},{10,11... | collective-permute-start | bytes 1179656 | tf_op jit(solution)/shard_map/ppermute | solution.py:377
  322.4 66.3 %collective-permute-start.8 = (bf16[1536,1024]{1,0:T(8,128)(2,1)}, bf16[1536,1024]{1,0:T(8,128)(2,1)}, u32[]{:S(2)}, u32[]{:S(2)}) collective-permute-start(bf16[1536,1024]{1,0:T(8,128)(2,1)} %collective-permute-done.1), channel_id=1, source_target_pairs={{0,2},{2,0},{4,6},{6,4},{8,10},{10,8},{12,14},{14,12},{16,18},{18,... | collective-permute-start | bytes 9437192 | tf_op jit(solution)/shard_map/ppermute | solution.py:388
  322.7 60.9 %collective-permute-start.9 = (bf16[1536,1024]{1,0:T(8,128)(2,1)}, bf16[1536,1024]{1,0:T(8,128)(2,1)}, u32[]{:S(2)}, u32[]{:S(2)}) collective-permute-start(bf16[1536,1024]{1,0:T(8,128)(2,1)} %collective-permute-done.4), channel_id=1, source_target_pairs={{0,2},{2,0},{4,6},{6,4},{8,10},{10,8},{12,14},{14,12},{16,18},{18,... | collective-permute-start | bytes 9437192 | tf_op jit(solution)/shard_map/ppermute | solution.py:388
  323.0 65.7 %collective-permute-start.10 = (bf16[1024,1536]{1,0:T(8,128)(2,1)}, bf16[1024,1536]{1,0:T(8,128)(2,1)}, u32[]{:S(2)}, u32[]{:S(2)}) collective-permute-start(bf16[1024,1536]{1,0:T(8,128)(2,1)} %collective-permute-done.5), channel_id=1, source_target_pairs={{0,2},{2,0},{4,6},{6,4},{8,10},{10,8},{12,14},{14,12},{16,18},{18,... | collective-permute-start | bytes 9437192 | tf_op jit(solution)/shard_map/ppermute | solution.py:388
  335.0 2.1 copy-start.10
  335.0 4.3 %slice-start = ((s8[6291456]{0:T(1024)(128)(4,1)}), s8[4194304]{0:T(1024)(128)(4,1)S(1)}, s32[]{:S(2)}) async-start(s8[6291456]{0:T(1024)(128)(4,1)} %bitcast.159), calls=%async_computation.2 | async-start | bytes 8388608
  337.1 2.2 slice-start.1
  338.9 0.7 copy-start.18
  397.9 4.3 %copy-start.1 = (bf16[1536,768]{1,0:T(8,128)(2,1)S(1)}, bf16[1536,768]{1,0:T(8,128)(2,1)}, u32[]{:S(2)}) copy-start(bf16[1536,768]{1,0:T(8,128)(2,1)} %param.20) | copy-start | bytes 7077892
Sparse Core Ops, SparseCore 0:
  15.9 131.2 all-gather.3
  148.8 128.5 all-gather.5

commit v3 on v2

--- a/solution.py
+++ b/solution.py
@@ -22,6 +22,7 @@
 QUERY_TILE = 256
 CACHE_BLOCK = 256
 SUM_ROWS = 16
+HIDDEN_TILE = 512
 
 
 def norm_rows(values, gain_vec):
@@ -240,6 +241,91 @@
     )(groups, lengths, queries, fresh_k, fresh_v, cache_k, cache_v, prompts)
 
 
+def finish_kernel(counts, *refs):
+    pair_count, set_count, tiles = counts
+    heads = [refs[2 * pair : 2 * pair + 2] for pair in range(pair_count)]
+    tokens_ref, gain_ref = refs[2 * pair_count : 2 * pair_count + 2]
+    refs = refs[2 * pair_count + 2 :]
+    sets = [refs[3 * index : 3 * index + 3] for index in range(set_count)]
+    out_ref, normed_ref, total_ref = refs[3 * set_count :]
+    step = pl.program_id(0)
+    requests, rows = tokens_ref.shape[:2]
+
+    @pl.when(step == 0)
+    def _():
+        for request in range(requests):
+            summed = tokens_ref[request].astype(jnp.float32)
+            for attended_ref, weight_ref in heads:
+                summed = summed + jnp.dot(
+                    attended_ref[request].T, weight_ref[...], preferred_element_type=jnp.float32
+                )
+            place = slice(request * rows, (request + 1) * rows)
+            residual = summed.astype(jnp.bfloat16)
+            normed_ref[place, :] = norm_rows(residual, gain_ref[...])
+            total_ref[place, :] = residual.astype(jnp.float32)
+
+    first = 0
+    for (gate_ref, up_ref, down_ref), count in zip(sets, tiles, strict=True):
+
+        @pl.when((step >= first) & (step < first + count))
+        def _(gate_ref=gate_ref, up_ref=up_ref, down_ref=down_ref):
+            normed = normed_ref[...]
+            gate = jnp.dot(normed, gate_ref[...], preferred_element_type=jnp.float32)
+            up = jnp.dot(normed, up_ref[...], preferred_element_type=jnp.float32)
+            hidden = (gate / (1.0 + jnp.exp(-gate)) * up).astype(jnp.bfloat16)
+            total_ref[...] += jnp.dot(hidden, down_ref[...], preferred_element_type=jnp.float32)
+
+        first += count
+
+    @pl.when(step == first - 1)
+    def _():
+        for request in range(requests):
+            out_ref[request] = total_ref[request * rows : (request + 1) * rows, :].astype(
+                jnp.bfloat16
+            )
+
+
+def finish(pairs, tokens, gain, sets):
+    requests, rows, width = tokens.shape
+    tile = min(HIDDEN_TILE, *(gate.shape[1] for gate, _, _ in sets))
+    tiles = [gate.shape[1] // tile for gate, _, _ in sets]
+    whole = lambda array: pl.BlockSpec(
+        array.shape, lambda step: (0,) * array.ndim, pipeline_mode=pl.Buffered(1)
+    )
+    operands, specs = [], []
+    for attended, weight in pairs:
+        operands += [attended, weight]
+        specs += [whole(attended), whole(weight)]
+    gain = gain.reshape(1, width)
+    operands += [tokens, gain]
+    specs += [whole(tokens), whole(gain)]
+    first = 0
+    for (gate, up, down), count in zip(sets, tiles, strict=True):
+        place = lambda step, first=first, count=count: jnp.clip(step - first, 0, count - 1)
+        operands += [gate, up, down]
+        specs += [
+            pl.BlockSpec((width, tile), lambda step, place=place: (0, place(step))),
+            pl.BlockSpec((width, tile), lambda step, place=place: (0, place(step))),
+            pl.BlockSpec((tile, width), lambda step, place=place: (place(step), 0)),
+        ]
+        first += count
+    return pl.pallas_call(
+        functools.partial(finish_kernel, (len(pairs), len(sets), tiles)),
+        grid=(first,),
+        in_specs=specs,
+        out_specs=pl.BlockSpec((requests, rows, width), lambda step: (0, 0, 0)),
+        out_shape=jax.ShapeDtypeStruct((requests, rows, width), jnp.bfloat16),
+        scratch_shapes=[
+            pltpu.VMEM((requests * rows, width), jnp.bfloat16),
+            pltpu.VMEM((requests * rows, width), jnp.float32),
+        ],
+        compiler_params=pltpu.CompilerParams(
+            dimension_semantics=("arbitrary",), vmem_limit_bytes=56 * 1024 * 1024
+        ),
+        name="finish",
+    )(*operands)
+
+
 def body(
     dp_size,
     tensor_size,
@@ -264,7 +350,7 @@
     query_cols = w_query.shape[1]
     key_cols = key_matrix.shape[1]
     key_heads = key_cols // HEAD_SIZE
-    paired = tensor_size == 2 and dp_size % 2 == 0
+    paired = tensor_size == 2 and dp_size % 2 == 0 and key_heads % 2 == 0
     swap = [(0, 1), (1, 0)]
     across = [(rank, rank ^ 1) for rank in range(dp_size)]
     tensor_rank = lax.axis_index("tensor")
@@ -341,21 +427,7 @@
     prompts += [lax.all_gather(part, "dp", axis=0) for part in parts[1:]]
 
     chunk_cols = query_cols // chunks
-    attn_part = jnp.zeros((local_reqs * local_rows, MODEL_WIDTH), jnp.float32)
-
-    def add_out(total, attended, weight):
-        return total + jnp.concatenate(
-            [
-                lax.dot_general(
-                    attended[request],
-                    weight,
-                    (((0,), (0,)), ((), ())),
-                    preferred_element_type=jnp.float32,
-                )
-                for request in range(local_reqs)
-            ]
-        )
-
+    pairs = []
     parts_of = lambda chunk: slice(chunk * chunk_cols, (chunk + 1) * chunk_cols)
     swapped = []
     for chunk in range(chunks):
@@ -376,38 +448,22 @@
             sent = lax.dynamic_slice_in_dim(attended, (1 - tensor_rank) * local_rows, local_rows, 2)
             swapped.append(lax.ppermute(sent, "tensor", swap))
             mine = lax.dynamic_slice_in_dim(attended, tensor_rank * local_rows, local_rows, 2)
-            attn_part = add_out(attn_part, mine, w_out[parts_of(chunk)])
+            pairs.append((mine, w_out[parts_of(chunk)]))
         else:
             spread = lax.all_to_all(attended, "tensor", split_axis=2, concat_axis=1, tiled=True)
             rows = weights[1].reshape(tensor_size, chunks, chunk_cols, MODEL_WIDTH)[:, chunk]
-            attn_part = add_out(
-                attn_part, spread, rows.reshape(tensor_size * chunk_cols, MODEL_WIDTH)
-            )
+            pairs.append((spread, rows.reshape(tensor_size * chunk_cols, MODEL_WIDTH)))
     hidden_sets = [(weights[0], *weights[2:])]
     if paired:
         passed = [lax.ppermute(part, "dp", across) for part in fetched]
         hidden_sets += [(fetched[0], *fetched[2:]), (passed[0], *passed[2:])]
         first_core = core == 0
-        other_out = jnp.concatenate(
-            [
-                jnp.where(first_core, fetched[1], passed[1]),
-                jnp.where(first_core, passed[1], fetched[1]),
-            ]
-        )
-        for chunk in range(chunks):
-            attn_part = add_out(attn_part, swapped[chunk], other_out[parts_of(chunk)])
-
-    own_tokens = tokens.transpose(1, 0, 2).reshape(local_reqs * local_rows, MODEL_WIDTH)
-    residual = (own_tokens.astype(jnp.float32) + attn_part).astype(jnp.bfloat16)
-    normed_mlp = norm_rows(residual, mlp_gain)
-    mlp_part = jnp.zeros((local_reqs * local_rows, MODEL_WIDTH), jnp.float32)
-    for gate, up, down in hidden_sets:
-        gate_part = jnp.dot(normed_mlp, gate, preferred_element_type=jnp.float32)
-        up_part = jnp.dot(normed_mlp, up, preferred_element_type=jnp.float32)
-        hidden = (jax.nn.silu(gate_part) * up_part).astype(jnp.bfloat16)
-        mlp_part = mlp_part + jnp.dot(hidden, down, preferred_element_type=jnp.float32)
-    result = (residual.astype(jnp.float32) + mlp_part).astype(jnp.bfloat16)
-    return result.reshape(local_reqs, local_rows, MODEL_WIDTH).transpose(1, 0, 2)
+        pairs += [
+            (jnp.where(first_core, swapped[0], swapped[1]), fetched[1]),
+            (jnp.where(first_core, swapped[1], swapped[0]), passed[1]),
+        ]
+    result = finish(pairs, tokens.transpose(1, 0, 2), mlp_gain, hidden_sets)
+    return result.transpose(1, 0, 2)
 
 
 def solution(mesh):

time: 414 us -> 383 us (0.925); the launches traced: 409 us -> 382 us
  matrix products: 78.9 us -> 9.75 us
  Pallas kernels: 71 us -> 102 us
  waiting for transfers between devices: 162 us -> 170 us
  local copies, waits for them, and re-layouts: 55.6 us -> 60.9 us
    dot_general x14 -> x0, matrix products: 65.8 us -> none  [the longest x3 33.3 us: body(): jnp.dot(hidden, down, preferred_element_type=jnp.float32)]
    pallas_call x0 -> x1, Pallas kernels: none -> 35.5 us  [finish(): pl.pallas_call(functools.partial(finish_kernel, (len(pairs), len(sets), t...]
    pallas_call x2, Pallas kernels: 71 us -> 66.3 us  [attend(): pl.pallas_call(attention_kernel, grid_spec=pltpu.PrefetchScalarGridSpec(n...]
    transpose x0 -> x1, local copies, waits for them, and re-layouts: none -> 4.32 us  [body(): return result.transpose(1, 0, 2)]
    unnamed x47 -> x53, local copies, waits for them, and re-layouts: 32.8 us -> 35.4 us
    dynamic_slice x3 -> x2, local copies, waits for them, and re-layouts: 12.7 us -> 10.6 us  [body(): sent.append(lax.dynamic_slice_in_dim(weight, core * half, half, axis))]
  transfers between devices with their start and end apart: 13 -> 13, of which waited for: 6 -> 7; matrix products, arithmetic and copies ran while one was open for 29% -> 16% of each run, Pallas kernels for 17% -> 17%
where the time goes in v3:
time: 383 us; the launch traced here: 382 us
  waiting for transfers between devices  170 us (44%)
  Pallas kernels  102 us (27%)
  local copies, waits for them, and re-layouts  60.9 us (16%)
  other arithmetic  15 us (4%)
  between operations  13.7 us (4%)
  starting transfers between devices  10.9 us (3%)
  matrix products  9.75 us (3%)
    all_gather x1, waiting for transfers between devices, body(): prompts += [lax.all_gather(part, 'dp', axis=0) for part in parts[1:]]  89.3 us
    pallas_call x2, Pallas kernels, attend(): pl.pallas_call(attention_kernel, grid_spec=pltpu.PrefetchScalarGridSpec(n...  66.3 us
    ppermute x1, waiting for transfers between devices, body(): fetched = [lax.ppermute(sent[0], 'tensor', swap)]  41 us
    pallas_call x1, Pallas kernels, finish(): pl.pallas_call(functools.partial(finish_kernel, (len(pairs), len(sets), t...  35.5 us
    unnamed x53, local copies, waits for them, and re-layouts  35.4 us
    all_gather x1, waiting for transfers between devices, body(): prompts = [lax.all_gather(parts[0], 'dp', axis=0)]  20.6 us
    ppermute x2, waiting for transfers between devices, body(): swapped.append(lax.ppermute(sent, 'tensor', swap))  13.7 us
    dynamic_slice x2, local copies, waits for them, and re-layouts, body(): sent.append(lax.dynamic_slice_in_dim(weight, core * half, half, axis))  10.6 us
  transfers between devices with their start and end apart: 13, of which 7 were waited for; matrix products, arithmetic and copies ran while one was open for 16% of the time, Pallas kernels for 17%

profile of v3, /device:TPU:0, one launch (start us, length us, event | category | flops | bytes accessed | tf_op | source)
XLA Modules:
  0.0 382.4 jit_solution(7069613490777772873)
XLA Ops:
  6.5 2.8 copy.42
  9.3 2.6 copy.43
  11.9 3.9 %pad_maximum_fusion.2 = (bf16[8,2,192,256]{3,2,1,0:T(8,128)(2,1)}, bf16[8,2,192,256]{3,2,1,0:T(8,128)(2,1)}) fusion(bf16[8,4,96,256]{3,2,1,0:T(8,128)(2,1)} %bitcast.105, bf16[8,4,96,256]{3,2,1,0:T(8,128)(2,1)} %bitcast.104), kind=kLoop, calls=%fused_computation.20 | loop fusion | flops 6291456 | bytes 6291456 | tf_op jit(solution)/shard_map/concatenate | solution.py:363
  15.9 1.9 fusion
  17.8 1.6 fusion.2
  19.4 3.0 collective-permute-start
  22.3 8.6 %copy.52 = bf16[2,4096,384]{1,2,0:T(8,128)(2,1)} copy(bf16[2,4096,384]{2,1,0:T(8,128)(2,1)} %param.24) | data formatting | bytes 12582912 | tf_op args[8]
  30.9 8.8 %copy.53 = bf16[2,4096,384]{1,2,0:T(8,128)(2,1)} copy(bf16[2,4096,384]{2,1,0:T(8,128)(2,1)} %param.25) | data formatting | bytes 12582912 | tf_op args[9]
  39.8 0.8 multiply_cosine_fusion
  40.6 3.9 %constant_dynamic-slice_fusion.4 = bf16[1024,1536]{1,0:T(8,128)(2,1)} fusion(bf16[2048,1536]{1,0:T(8,128)(2,1)} %refs_12_.1, s32[]{:T(128)S(6)} %select_n.49), kind=kLoop, calls=%fused_computation.53 | loop fusion | bytes 6291460 | tf_op jit(solution)/shard_map/dynamic_slice | solution.py:380
  44.5 6.6 %constant_dynamic-slice_fusion.5 = (bf16[1536,1024]{1,0:T(8,128)(2,1)}, bf16[1536,1024]{1,0:T(8,128)(2,1)}) fusion(bf16[1536,2048]{1,0:T(8,128)(2,1)} %refs_11_.1, s32[]{:T(128)S(6)} %select_n.49, bf16[1536,2048]{1,0:T(8,128)(2,1)} %refs_10_.1), kind=kLoop, calls=%fused_computation.54 | loop fusion | bytes 12582916 | tf_op jit(solution)/shard_map/dynamic_slice | solution.py:380
  51.1 1.8 fusion.19
  53.0 4.1 %collective-permute-done = bf16[2,256,1536]{2,1,0:T(8,128)(2,1)} collective-permute-done((bf16[2,256,1536]{2,1,0:T(8,128)(2,1)}, bf16[2,256,1536]{2,1,0:T(8,128)(2,1)}, u32[]{:S(2)}, u32[]{:S(2)}) %collective-permute-start) | collective-permute-done | bytes 1572896 | tf_op jit(solution)/shard_map/ppermute | solution.py:376
  57.0 1.7 collective-permute-start.1
  58.8 2.2 broadcast_select_fusion.1
  61.0 1.1 copy-done.9
  62.7 2.5 convolution_bitcast_fusion
  65.2 3.1 copy.46
  68.3 1.5 fusion.6
  69.8 1.1 copy-done.17
  70.9 2.5 convolution_bitcast_fusion.1
  73.5 3.3 copy.45
  76.7 2.2 fusion.11
  79.0 0.8 fusion.10
  80.3 1.1 copy-done.13
  81.4 0.8 fusion.16
  82.2 0.8 fusion.20
  83.4 1.1 copy-done.14
  85.7 41.0 %collective-permute-done.1.refs_13_ = bf16[1536,1024]{1,0:T(8,128)(2,1)} collective-permute-done((bf16[1536,1024]{1,0:T(8,128)(2,1)}, bf16[1536,1024]{1,0:T(8,128)(2,1)}, u32[]{:S(2)}, u32[]{:S(2)}) %collective-permute-start.1) | collective-permute-done | bytes 3145760 | tf_op jit(solution)/shard_map/ppermute | solution.py:382
  126.6 20.6 %all-gather.4.cloned.1.call-done.prompt_ref = bf16[16,8,384,256]{3,2,1,0:T(8,128)(2,1)} async-done(((bf16[1,8,384,256]{3,2,1,0:T(8,128)(2,1)}), bf16[16,8,384,256]{3,2,1,0:T(8,128)(2,1)}) %all-gather.4.cloned.1.call-update) | async-done | bytes 25165840 | tf_op jit(solution)/shard_map/all_gather | solution.py:370
  147.3 1.5 collective-permute-start.4
  149.4 1.5 collective-permute-start.3
  150.8 2.8 copy-done.2
  153.6 33.5 %attend.2 = bf16[2,384,512]{2,1,0:T(8,128)(2,1)S(1)} custom-call(s32[2]{0:T(128)S(1)} %copy-done.4, s32[2]{0:T(128)S(1)} %copy-done.5, bf16[2,768,512]{2,1,0:T(8,128)(2,1)S(1)} %bitcast.91, bf16[2,384,512]{2,1,0:T(8,128)(2,1)S(1)} %bitcast.93, bf16[2,384,512]{2,1,0:T(8,128)(2,1)S(1)} %pad_maximum_fusion.6.fresh_v_ref, bf16[2,384,4096]{2,1,0:T(8,128)(2,1)S(1)} %bitcast.89, ...), custom_call_target="tpu_custom_call" | custom-call | flops 1 | bytes 1 | tf_op jit(solution)/shard_map/attend/pallas_call | solution.py:212
  187.1 1.0 constant_dynamic-slice_fusion.2
  188.1 89.3 %all-gather.6.cloned.1.call-done = bf16[128,384,256]{2,1,0:T(8,128)(2,1)} async-done(((bf16[8,384,256]{2,1,0:T(8,128)(2,1)}), bf16[128,384,256]{2,1,0:T(8,128)(2,1)}) %all-gather.6.cloned.1.call-update) | async-done | bytes 25165840 | tf_op jit(solution)/shard_map/all_gather | solution.py:427
  277.4 2.8 copy-done.3
  280.2 32.8 %attend.3 = bf16[2,384,512]{2,1,0:T(8,128)(2,1)S(1)} custom-call(s32[2]{0:T(128)S(1)} %copy-done.4, s32[2]{0:T(128)S(1)} %copy-done.5, bf16[2,768,512]{2,1,0:T(8,128)(2,1)S(1)} %bitcast.92, bf16[2,384,512]{2,1,0:T(8,128)(2,1)S(1)} %bitcast.94, bf16[2,384,512]{2,1,0:T(8,128)(2,1)S(1)} %pad_maximum_fusion.6.fresh_v_ref, bf16[2,384,4096]{2,1,0:T(8,128)(2,1)S(1)} %bitcast.90, ...), custom_call_target="tpu_custom_call" | custom-call | flops 1 | bytes 1 | tf_op jit(solution)/shard_map/attend/pallas_call | solution.py:212
  313.0 5.9 %collective-permute-done.2 = bf16[2,384,256]{2,1,0:T(8,128)(2,1)S(1)} collective-permute-done((bf16[2,384,256]{2,1,0:T(8,128)(2,1)}, bf16[2,384,256]{2,1,0:T(8,128)(2,1)S(1)}, u32[]{:S(2)}, u32[]{:S(2)}) %collective-permute-start.2) | collective-permute-done | bytes 393248 | tf_op jit(solution)/shard_map/ppermute | solution.py:449
  320.0 0.8 constant_dynamic-slice_fusion
  320.8 1.5 collective-permute-start.6
  322.3 1.3 copy.68
  323.6 0.6 reshape.74.refs_9_
  324.2 7.8 %collective-permute-done.6 = bf16[2,384,256]{2,1,0:T(8,128)(2,1)} collective-permute-done((bf16[2,384,256]{2,1,0:T(8,128)(2,1)S(1)}, bf16[2,384,256]{2,1,0:T(8,128)(2,1)}, u32[]{:S(2)}, u32[]{:S(2)}) %collective-permute-start.6) | collective-permute-done | bytes 393248 | tf_op jit(solution)/shard_map/ppermute | solution.py:449
  332.0 2.0 broadcast_select_fusion.2
  334.1 1.6 collective-permute-done.10.refs_18_
  335.7 35.5 %finish.1 = bf16[2,256,1536]{2,1,0:T(8,128)(2,1)} custom-call(bf16[2,384,256]{2,1,0:T(8,128)(2,1)} %get-tuple-element.65.refs_0_, bf16[384,1536]{1,0:T(8,128)(2,1)} %get-tuple-element.57.refs_1_, bf16[2,384,256]{2,1,0:T(8,128)(2,1)} %get-tuple-element.63.refs_2_, bf16[384,1536]{1,0:T(8,128)(2,1)} %get-tuple-element.55.refs_3_, ...), custom_call_target="tpu_custom_call" | custom-call | tf_op jit(solution)/shard_map/finish/pallas_call | solution.py:312
  371.2 4.3 %copy.54 = bf16[256,2,1536]{2,1,0:T(2,128)(2,1)} copy(bf16[256,2,1536]{2,0,1:T(8,128)(2,1)} %bitcast.99) | data formatting | bytes 3145728 | tf_op jit(solution)/shard_map/transpose | solution.py:466
  (67 shorter events, 4.4 us)
Async XLA Ops:
  6.5 56.2 %copy-start = (bf16[1536,768]{1,0:T(8,128)(2,1)S(1)}, bf16[1536,768]{1,0:T(8,128)(2,1)}, u32[]{:S(2)}) copy-start(bf16[1536,768]{1,0:T(8,128)(2,1)} %param.20) | copy-start | bytes 7077892
  6.5 140.7 %all-gather.4.cloned.1.call-start = ((), (), s32[]{:S(2)}) async-start(), calls=%async_computation | async-start | bytes 26738688 | tf_op jit(solution)/shard_map/all_gather | solution.py:370
  15.8 2.0 copy-start.21
  15.8 261.7 %all-gather.6.cloned.1.call-start = ((), (), s32[]{:S(2)}) async-start(), calls=%async_computation.1 | async-start | bytes 26738688 | tf_op jit(solution)/shard_map/all_gather | solution.py:427
  15.8 1.9 copy-start.6
  19.4 37.7 %collective-permute-start = (bf16[2,256,1536]{2,1,0:T(8,128)(2,1)}, bf16[2,256,1536]{2,1,0:T(8,128)(2,1)}, u32[]{:S(2)}, u32[]{:S(2)}) collective-permute-start(bf16[2,256,1536]{2,1,0:T(8,128)(2,1)} %fusion.2), channel_id=1, source_target_pairs={{0,1},{1,0},{2,3},{3,2},{4,5},{5,4},{6,7},{7,6},{8,9},{9,8},{10,11... | collective-permute-start | bytes 4718600 | tf_op jit(solution)/shard_map/ppermute | solution.py:376
  30.9 8.8 %copy-start.5 = (s32[2]{0:T(128)S(1)}, s32[2]{0:T(128)}, u32[]{:S(2)}) copy-start(s32[2]{0:T(128)} %len_ref.3) | copy-start | bytes 28
  44.5 6.6 %copy-start.16 = (bf16[768,1536]{1,0:T(8,128)(2,1)S(1)}, bf16[768,1536]{1,0:T(8,128)(2,1)}, u32[]{:S(2)}) copy-start(bf16[768,1536]{1,0:T(8,128)(2,1)} %param.23) | copy-start | bytes 7077892
  51.1 7.7 %copy-start.7 = (bf16[256,2,1536]{2,1,0:T(2,128)(2,1)S(1)}, bf16[256,2,1536]{2,1,0:T(2,128)(2,1)}, u32[]{:S(2)}) copy-start(bf16[256,2,1536]{2,1,0:T(2,128)(2,1)} %param.16) | copy-start | bytes 4718596
  57.0 69.6 %collective-permute-start.1 = (bf16[1536,1024]{1,0:T(8,128)(2,1)}, bf16[1536,1024]{1,0:T(8,128)(2,1)}, u32[]{:S(2)}, u32[]{:S(2)}) collective-permute-start(bf16[1536,1024]{1,0:T(8,128)(2,1)} %get-tuple-element.28), channel_id=1, source_target_pairs={{0,1},{1,0},{2,3},{3,2},{4,5},{5,4},{6,7},{7,6},{8,9},{9,8},{10,11... | collective-permute-start | bytes 9437192 | tf_op jit(solution)/shard_map/ppermute | solution.py:382
  61.0 1.2 copy-start.9
  61.0 1.7 copy-start.11
  69.8 1.2 copy-start.17
  73.5 3.3 copy-start.10
  73.5 3.3 copy-start.12
  76.7 2.3 copy-start.18
  76.7 2.3 copy-start.23
  79.0 1.3 copy-start.20
  79.8 1.5 copy-start.13
  83.0 1.4 copy-start.14
  83.0 1.9 copy-start.15
  85.7 65.2 %copy-start.4 = (s32[2]{0:T(128)S(1)}, s32[2]{0:T(128)}, u32[]{:S(2)}) copy-start(s32[2]{0:T(128)} %group_ref.3) | copy-start | bytes 28
  147.3 171.7 %collective-permute-start.4 = (bf16[1536,1024]{1,0:T(8,128)(2,1)}, bf16[1536,1024]{1,0:T(8,128)(2,1)}, u32[]{:S(2)}, u32[]{:S(2)}) collective-permute-start(bf16[1536,1024]{1,0:T(8,128)(2,1)} %get-tuple-element.41), channel_id=1, source_target_pairs={{0,1},{1,0},{2,3},{3,2},{4,5},{5,4},{6,7},{7,6},{8,9},{9,8},{10,11... | collective-permute-start | bytes 9437192 | tf_op jit(solution)/shard_map/ppermute | solution.py:423
  148.8 170.1 %collective-permute-start.5 = (bf16[1024,1536]{1,0:T(8,128)(2,1)}, bf16[1024,1536]{1,0:T(8,128)(2,1)}, u32[]{:S(2)}, u32[]{:S(2)}) collective-permute-start(bf16[1024,1536]{1,0:T(8,128)(2,1)} %constant_dynamic-slice_fusion.4), channel_id=1, source_target_pairs={{0,1},{1,0},{2,3},{3,2},{4,5},{5,4},{6,7},{7,6},{8,9},{9,8},{10,11... | collective-permute-start | bytes 9437192 | tf_op jit(solution)/shard_map/ppermute | solution.py:423
  149.4 169.6 %collective-permute-start.3 = (bf16[384,1536]{1,0:T(8,128)(2,1)}, bf16[384,1536]{1,0:T(8,128)(2,1)}, u32[]{:S(2)}, u32[]{:S(2)}) collective-permute-start(bf16[384,1536]{1,0:T(8,128)(2,1)} %get-tuple-element.40), channel_id=1, source_target_pairs={{0,1},{1,0},{2,3},{3,2},{4,5},{5,4},{6,7},{7,6},{8,9},{9,8},{10,11... | collective-permute-start | bytes 3538952 | tf_op jit(solution)/shard_map/ppermute | solution.py:423
  150.8 2.8 copy-start.2
  188.1 130.8 %collective-permute-start.2 = (bf16[2,384,256]{2,1,0:T(8,128)(2,1)}, bf16[2,384,256]{2,1,0:T(8,128)(2,1)S(1)}, u32[]{:S(2)}, u32[]{:S(2)}) collective-permute-start(bf16[2,384,256]{2,1,0:T(8,128)(2,1)} %get-tuple-element.64), channel_id=1, source_target_pairs={{0,1},{1,0},{2,3},{3,2},{4,5},{5,4},{6,7},{7,6},{8,9},{9,8},{10,11... | collective-permute-start | bytes 1179656 | tf_op jit(solution)/shard_map/ppermute | solution.py:449
  277.4 2.8 copy-start.3
  313.0 9.3 %copy-start.8 = (bf16[256,2,1536]{2,1,0:T(2,128)(2,1)S(1)}, bf16[256,2,1536]{2,1,0:T(2,128)(2,1)}, u32[]{:S(2)}) copy-start(bf16[256,2,1536]{2,1,0:T(2,128)(2,1)} %param.16) | copy-start | bytes 4718596
  318.9 15.1 %collective-permute-start.8 = (bf16[1536,1024]{1,0:T(8,128)(2,1)}, bf16[1536,1024]{1,0:T(8,128)(2,1)}, u32[]{:S(2)}, u32[]{:S(2)}) collective-permute-start(bf16[1536,1024]{1,0:T(8,128)(2,1)} %collective-permute-done.1.refs_13_), channel_id=1, source_target_pairs={{0,2},{2,0},{4,6},{6,4},{8,10},{10,8},{12,14},{14,12},{16,18},{18,... | collective-permute-start | bytes 9437192 | tf_op jit(solution)/shard_map/ppermute | solution.py:458
  319.0 15.0 %collective-permute-start.9 = (bf16[1536,1024]{1,0:T(8,128)(2,1)}, bf16[1536,1024]{1,0:T(8,128)(2,1)}, u32[]{:S(2)}, u32[]{:S(2)}) collective-permute-start(bf16[1536,1024]{1,0:T(8,128)(2,1)} %collective-permute-done.4.refs_14_), channel_id=1, source_target_pairs={{0,2},{2,0},{4,6},{6,4},{8,10},{10,8},{12,14},{14,12},{16,18},{18,... | collective-permute-start | bytes 9437192 | tf_op jit(solution)/shard_map/ppermute | solution.py:458
  319.5 16.2 %collective-permute-start.10 = (bf16[1024,1536]{1,0:T(8,128)(2,1)}, bf16[1024,1536]{1,0:T(8,128)(2,1)}, u32[]{:S(2)}, u32[]{:S(2)}) collective-permute-start(bf16[1024,1536]{1,0:T(8,128)(2,1)} %collective-permute-done.5.refs_15_), channel_id=1, source_target_pairs={{0,2},{2,0},{4,6},{6,4},{8,10},{10,8},{12,14},{14,12},{16,18},{18,... | collective-permute-start | bytes 9437192 | tf_op jit(solution)/shard_map/ppermute | solution.py:458
  319.6 14.5 %collective-permute-start.7 = (bf16[384,1536]{1,0:T(8,128)(2,1)}, bf16[384,1536]{1,0:T(8,128)(2,1)S(1)}, u32[]{:S(2)}, u32[]{:S(2)}) collective-permute-start(bf16[384,1536]{1,0:T(8,128)(2,1)} %collective-permute-done.3.refs_5_), channel_id=1, source_target_pairs={{0,2},{2,0},{4,6},{6,4},{8,10},{10,8},{12,14},{14,12},{16,18},{18,... | collective-permute-start | bytes 3538952 | tf_op jit(solution)/shard_map/ppermute | solution.py:458
  320.8 11.2 %collective-permute-start.6 = (bf16[2,384,256]{2,1,0:T(8,128)(2,1)S(1)}, bf16[2,384,256]{2,1,0:T(8,128)(2,1)}, u32[]{:S(2)}, u32[]{:S(2)}) collective-permute-start(bf16[2,384,256]{2,1,0:T(8,128)(2,1)S(1)} %get-tuple-element.62), channel_id=1, source_target_pairs={{0,1},{1,0},{2,3},{3,2},{4,5},{5,4},{6,7},{7,6},{8,9},{9,8},{10,11... | collective-permute-start | bytes 1179656 | tf_op jit(solution)/shard_map/ppermute | solution.py:449
  322.3 1.3 copy-start.22
  334.1 1.6 copy-start.19
  371.2 4.3 %copy-start.1 = (bf16[1536,768]{1,0:T(8,128)(2,1)S(1)}, bf16[1536,768]{1,0:T(8,128)(2,1)}, u32[]{:S(2)}) copy-start(bf16[1536,768]{1,0:T(8,128)(2,1)} %param.20) | copy-start | bytes 7077892
Sparse Core Ops, SparseCore 0:
  15.9 131.2 all-gather.3
  148.8 128.5 all-gather.5
